TPU v7x, 256 devices: a whole 4x4x8 slice. The times are simulated.
256 devices in a mesh: ctx: 64 (over z_lo, x, y, core), dp: 4 (over z_hi).
Axes of the slice: x: 4, y: 4, z: 8 (z_hi: 4, z_lo: 2; z = z_hi * 2 + z_lo), core: 2. Of those that a mesh axis runs over, the one named last changes fastest.
Arguments:
- hidden: bfloat16 [4, 8192, 1024], P('dp', 'ctx'), may hold values from -6 to 6
- depth: int32 [4, 8192], P('dp', 'ctx'), may hold values from 1 to 3, as said below
- cotangent: bfloat16 [4, 8192, 1024], P('dp', 'ctx'), may hold values from -6 to 6
- embeds: float32 [2, 1024], replicated, may hold values from -4 to 4
- mods: float32 [2, 3, 1024], replicated, may hold values from -4 to 4
- w_query: bfloat16 [1024, 1024], replicated, may hold values from -0.1875 to 0.1875
- w_key: bfloat16 [1024, 1024], replicated, may hold values from -0.1875 to 0.1875
- w_value: bfloat16 [1024, 1024], replicated, may hold values from -0.1875 to 0.1875
- w_out: bfloat16 [1024, 1024], replicated, may hold values from -0.1875 to 0.1875
Outputs:
- grad_hidden: bfloat16 [4, 8192, 1024], P('dp', 'ctx')
- grad_query: float32 [1024, 1024], P('ctx')
- grad_key: float32 [1024, 1024], P('ctx')
- grad_value: float32 [1024, 1024], P('ctx')
- grad_out: float32 [1024, 1024], P('ctx')
- grad_embeds: float32 [2, 1024], replicated
- grad_mods: float32 [2, 3, 1024], replicated
Inputs may be any that keep to these rules, and one draw needn't show every extreme that they name: Within the tokens of one device (each aligned block of 128 positions) between 6 and 12 tokens have depth 2 or more, exactly 12 in at least one block of every draw; each block holds at least one token of depth 3.
All inputs are finite; a program needn't handle non-finite values.
Results may differ from a plain program's by a relative error of at most 0.028.
Values may be sent and summed in bfloat16 or wider, within the bound.
No kernel may reach another device: no remote copies, remote signals or barrier semaphores. Data moves between devices by JAX's collectives and lax.ppermute only.
A program may use at most 128 MiB of HBM per device.

v0:
```python
import jax
import jax.numpy as jnp
from jax import lax
from jax.experimental import pallas as pl
from jax.experimental.pallas import tpu as pltpu
from jax.sharding import Mesh, PartitionSpec as P

D = 1024
H = 8
DH = 128
TOK = 128
CAP = 12
N_CTX = 64
CHIPS = 32
SLOTS = 768
HALF = 512
HEADS = 4
FORWARD_HEADS = 4
BACKWARD_HEADS = 4
TILES = 24
PACKED = (TILES + 1) * 8
BLK = 256
NBLK = SLOTS // BLK
EPSILON = 1e-06
NEGATIVE = -1e30
EMPTY = 64.0
SCALE = DH ** (-0.5)
SCALE2 = SCALE * 1.4426950408889634
BF = jnp.bfloat16
F32 = jnp.float32

VSPEC = pl.BlockSpec(memory_space=pltpu.VMEM)
LOAD = pl.BlockSpec(memory_space=pltpu.VMEM)
HSPEC = pl.BlockSpec(memory_space=pl.ANY)


def nn(a, b):
    return lax.dot_general(a, b, (((1,), (0,)), ((), ())), preferred_element_type=F32)


def nt(a, b):
    return lax.dot_general(a, b, (((1,), (1,)), ((), ())), preferred_element_type=F32)


def tn(a, b):
    return lax.dot_general(a, b, (((0,), (0,)), ((), ())), preferred_element_type=F32)


def sds(shape, dtype):
    return jax.ShapeDtypeStruct(shape, dtype)


def call(kernel, outs, in_specs, scratch=(), vmem=16, pinned=True):
    if pinned:
        outs = tuple(pltpu.VMEM(s.shape, s.dtype) for s in outs)
    run = pl.pallas_call(
        kernel,
        out_shape=outs,
        in_specs=in_specs,
        out_specs=tuple(VSPEC for _ in outs),
        scratch_shapes=list(scratch),
        compiler_params=pltpu.CompilerParams(vmem_limit_bytes=vmem * 1024 * 1024),
    )

    def placed(*args):
        spaces = [pltpu.VMEM if spec is VSPEC else pltpu.HBM for spec in in_specs]
        return run(*(pltpu.with_memory_space_constraint(a, m) for a, m in zip(args, spaces)))

    return placed


def pick_kernel(depth_ref, hidden_ref, cot_ref, payload_ref, picker_ref, rows_ref, both):
    depth = jnp.broadcast_to(depth_ref[...], (16, TOK))
    active = depth >= 2
    before = lax.broadcasted_iota(jnp.int32, (TOK, TOK), 0)
    upto = lax.broadcasted_iota(jnp.int32, (TOK, TOK), 1)
    upper = jnp.where(before <= upto, 1.0, 0.0).astype(BF)
    placing = nn(jnp.where(active, 1.0, 0.0).astype(BF), upper) - 1.0
    slot = lax.broadcasted_iota(jnp.int32, (16, TOK), 0)
    hit = active & (placing == slot.astype(F32)) & (slot < CAP)
    picker = jnp.where(hit, 1.0, 0.0)
    picker_ref[...] = picker.astype(BF)
    level = jnp.sum(picker * (depth - 1).astype(F32), axis=1, keepdims=True)
    rows = nn(picker.astype(BF), hidden_ref[0])
    both[0:CAP] = jnp.where(level > 0.5, rows, EMPTY)[0:CAP]
    both[CAP : 2 * CAP] = nn(picker.astype(BF), cot_ref[0])[0:CAP]
    lane = lax.broadcasted_iota(jnp.int32, (8, 128), 1)
    level = jnp.broadcast_to(level, (16, 128))
    tiles = [both[8 * r : 8 * r + 8, 128 * c : 128 * c + 128] for r in range(3) for c in range(8)]
    tiles.append(jnp.where(lane < 64, level[0:8], level[8:16]))
    payload_ref[...] = jnp.concatenate(tiles, axis=0).astype(BF)
    rows_ref[...] = both[0:16].astype(BF)


def pick(depth, hidden, cotangent):
    return call(
        pick_kernel,
        (sds((PACKED, 128), BF), sds((16, TOK), BF), sds((16, D), BF)),
        [LOAD, LOAD, LOAD],
        [pltpu.VMEM((2 * CAP, D), F32)],
    )(depth, hidden, cotangent)


def causal_bias():
    key = lax.broadcasted_iota(jnp.int32, (BLK, BLK), 0)
    query = lax.broadcasted_iota(jnp.int32, (BLK, BLK), 1)
    return jnp.where(key <= query, 0.0, NEGATIVE).astype(F32)


def norm_rows(u):
    factor = lax.rsqrt(jnp.mean(u * u, axis=-1, keepdims=True) + EPSILON)
    return factor, u * factor


def biased_scores(k, q, bias_ref, causal, upto):
    s = nt(k, q)
    bias = bias_ref[0:upto, :]
    s = s + jnp.concatenate([bias, bias], axis=1)
    last = s[upto - BLK : upto] + causal
    if upto == BLK:
        return last
    return jnp.concatenate([s[: upto - BLK], last], axis=0)


def row_blocks(body, carry=0):
    def step(block, carry):
        return body(pl.ds(pl.multiple_of(block * BLK, BLK), BLK), carry)

    return lax.fori_loop(0, NBLK, step, carry)


def head_cols(head):
    return pl.ds(pl.multiple_of(head * DH, DH), DH)


def attention_forward(q_ref, k_ref, v_ref, o_ref, lse_ref, bias_ref):
    causal = causal_bias()
    ones = jnp.ones((16, SLOTS), BF)

    def some_heads(step, carry):
        items = []
        for part in range(FORWARD_HEADS):
            head = step * FORWARD_HEADS + part
            cols = head_cols(head)
            vt = jnp.concatenate([v_ref[:, cols].T, ones], axis=0)
            items += [(head, cols, vt, block) for block in range(NBLK)]

        def start(head, cols, vt, block):
            upto = (block + 1) * BLK
            s = biased_scores(k_ref[0:upto, cols], q_ref[block * BLK : upto, cols], bias_ref, causal, upto)
            return s, jnp.max(s, axis=0, keepdims=True)

        def finish(head, cols, vt, block, s, top):
            upto = (block + 1) * BLK
            rows = slice(block * BLK, upto)
            e = jnp.exp2((s - top) * SCALE2).astype(BF)
            both = nn(vt[:, 0:upto], e)
            total = both[DH : DH + 1]
            o_ref[rows, cols] = (both[0:DH] * (1.0 / total)).T.astype(BF)
            lse_ref[pl.ds(head, 1), rows] = jnp.maximum(top * SCALE2 + jnp.log2(total), -1e25)

        state = start(*items[0])
        for i, item in enumerate(items):
            following = start(*items[i + 1]) if i + 1 < len(items) else None
            finish(*item, *state)
            state = following
        return carry

    lax.fori_loop(0, HEADS // FORWARD_HEADS, some_heads, 0)


def attention_backward(
    q_ref, k_ref, v_ref, o_ref, do_ref, lse_ref, bias_ref, dq_ref, dk_ref, dv_ref, ps, dss
):
    causal = causal_bias()

    def some_heads(step, carry):
        items = []
        for part in range(BACKWARD_HEADS):
            head = step * BACKWARD_HEADS + part
            cols = head_cols(head)
            kt = k_ref[:, cols].T
            items += [(head, part % 2, cols, kt, block) for block in range(NBLK)]

        def start(head, slot, cols, kt, block):
            upto = (block + 1) * BLK
            rows = slice(block * BLK, upto)
            s = biased_scores(k_ref[0:upto, cols], q_ref[rows, cols], bias_ref, causal, upto)
            return s, nt(v_ref[0:upto, cols], do_ref[rows, cols])

        def finish(head, slot, cols, kt, block, s, dp):
            upto = (block + 1) * BLK
            rows = slice(block * BLK, upto)
            product = do_ref[rows, cols].astype(F32) * o_ref[rows, cols].astype(F32)
            inner = jnp.sum(product.T, axis=0, keepdims=True)
            p = jnp.exp2(s * SCALE2 - lse_ref[pl.ds(head, 1), rows])
            ds = (p * (dp - inner)).astype(BF)
            ps[slot, 0:upto, rows] = p.astype(BF)
            dss[slot, 0:upto, rows] = ds
            dq_ref[rows, cols] = (nn(kt[:, 0:upto], ds).T * SCALE).astype(BF)

        def close(head, slot, cols):
            for block in range(NBLK):
                rows = slice(block * BLK, (block + 1) * BLK)
                later = slice(block * BLK, SLOTS)
                dv_ref[rows, cols] = nn(ps[slot, rows, later], do_ref[later, cols]).astype(BF)
                dk_ref[rows, cols] = (nn(dss[slot, rows, later], q_ref[later, cols]) * SCALE).astype(BF)

        state = start(*items[0])
        for i, item in enumerate(items):
            following = start(*items[i + 1]) if i + 1 < len(items) else None
            finish(*item, *state)
            state = following
            if item[-1] == NBLK - 1:
                close(*item[:3])
        return carry

    lax.fori_loop(0, HEADS // BACKWARD_HEADS, some_heads, 0)


def project(x, rows, wq, wk, wv, q_ref, k_ref, v_ref):
    q_ref[rows, :] = nn(x, wq[...]).astype(BF)
    k_ref[rows, :] = nn(x, wk[...]).astype(BF)
    v_ref[rows, :] = nn(x, wv[...]).astype(BF)


def unproject(rows, wq, wk, wv, dq_ref, dk_ref, dv_ref):
    return nt(dq_ref[rows, :], wq[...]) + nt(dk_ref[rows, :], wk[...]) + nt(dv_ref[rows, :], wv[...])


def place_block(block_ref, chip, base, start, hs, gs, level):
    tiles = block_ref[chip].astype(F32)
    rows_h = hs.at[pl.ds(base, 2 * CAP)]
    rows_g = gs.at[pl.ds(base, 2 * CAP)]
    rows_level = level.at[pl.ds(base, 2 * CAP)]
    for c in range(8):
        cols = slice(128 * c, 128 * c + 128)
        upper, middle, lower = (tiles[8 * (8 * r + c) : 8 * (8 * r + c) + 8] for r in range(3))
        rows_h[start : start + 8, cols] = upper
        rows_h[start + 8 : start + 12, cols] = middle[0:4]
        rows_g[start : start + 4, cols] = middle[4:8]
        rows_g[start + 4 : start + 12, cols] = lower
    depths = tiles[8 * TILES :]
    turned = pltpu.roll(depths, 64, 1)
    lane = lax.broadcasted_iota(jnp.int32, (8, 128), 1)
    rows_level[start : start + 8] = jnp.where(lane < 64, depths, turned)
    rows_level[start + 8 : start + 12] = jnp.where(lane < 64, turned, depths)[0:4]


def weight_grads(core, chip, x_ref, o_ref, dy_ref, dq_ref, dk_ref, dv_ref, grads):
    strip = pl.multiple_of((chip // 4) * DH, DH)
    xs = x_ref[:, pl.ds(strip, DH)]
    grads[:, 0:HALF] = tn(xs, dq_ref[...])
    grads[:, HALF : 2 * HALF] = tn(xs, dk_ref[...])
    grads[:, 2 * HALF : 3 * HALF] = tn(xs, dv_ref[...])
    own = jnp.where(chip // 16 == core, 1.0, 0.0).astype(F32)
    o_strip = pl.multiple_of(((chip // 4) % 4) * DH, DH)
    os = o_ref[:, pl.ds(o_strip, DH)]
    grads[:, 3 * HALF :] = tn(os, dy_ref[...]) * own


def first_kernel(
    own_ref, other_ref, embeds_ref, mods_ref, wq_hbm, wk_hbm, wv_hbm, wo_hbm,
    q_ref, k_ref, v_ref, o_ref, lse_ref, h_ref, g_ref, level_ref, x_ref, wq, wk, wv, wo,
    hs, gs, bias, sems,
):
    core = lax.axis_index("core")
    half = pl.ds(pl.multiple_of(core * HALF, HALF), HALF)
    copies = [
        pltpu.make_async_copy(source.at[:, half], target, sems.at[i])
        for i, (source, target) in enumerate(((wq_hbm, wq), (wk_hbm, wk), (wv_hbm, wv)))
    ]
    copies.append(pltpu.make_async_copy(wo_hbm, wo, sems.at[3]))
    for copy in copies:
        copy.start()

    def place(even_ref, odd_ref):
        def one_chip(chip, carry):
            base = pl.multiple_of(chip * 2 * CAP, 8)
            place_block(even_ref, chip, base, 0, hs, gs, level_ref)
            place_block(odd_ref, chip, base, CAP, hs, gs, level_ref)
            return carry

        lax.fori_loop(0, CHIPS, one_chip, 0)

    @pl.when(core == 0)
    def _():
        place(own_ref, other_ref)

    @pl.when(core == 1)
    def _():
        place(other_ref, own_ref)

    bias[...] = jnp.where(level_ref[...] > 0.5, 0.0, NEGATIVE)
    for copy in copies:
        copy.wait()
    embed = embeds_ref[0:1, :]
    shift = mods_ref[0, 0:1, :]
    scale = 1.0 + mods_ref[1, 0:1, :]

    def norm_block(rows):
        h = hs[rows, :]
        g_ref[rows, :] = gs[rows, :].astype(BF)
        h_ref[rows, :] = h.astype(BF)
        factor, normed = norm_rows(h + embed)
        x_ref[rows, :] = (normed * scale + shift).astype(BF)

    norm_block(pl.ds(0, BLK))
    for block in range(NBLK):
        if block + 1 < NBLK:
            norm_block(pl.ds((block + 1) * BLK, BLK))
        rows = pl.ds(block * BLK, BLK)
        project(x_ref[rows, :], rows, wq, wk, wv, q_ref, k_ref, v_ref)
    attention_forward(q_ref, k_ref, v_ref, o_ref, lse_ref, bias)


def first(own, other, embeds, mods, wq, wk, wv, wo):
    half = sds((SLOTS, HALF), BF)
    full = sds((SLOTS, D), BF)
    return call(
        first_kernel,
        (half, half, half, half, sds((8, SLOTS), F32), full, full, sds((SLOTS, 128), F32), full)
        + (sds((D, HALF), BF),) * 3
        + (sds((D, D), BF),),
        [VSPEC] * 4 + [HSPEC] * 4,
        [
            pltpu.VMEM((SLOTS, D), F32),
            pltpu.VMEM((SLOTS, D), F32),
            pltpu.VMEM((SLOTS, 128), F32),
            pltpu.SemaphoreType.DMA((4,)),
        ],
        16,
    )(own, other, embeds, mods, wq, wk, wv, wo)


def upstream_kernel(g_ref, level_ref, mods_ref, wo, dy_ref, do_ref):
    core = lax.axis_index("core")
    own_rows = pl.ds(pl.multiple_of(core * HALF, HALF), HALF)
    gate1 = mods_ref[2, 1:2, :]

    def some_rows(rows, carry):
        deep = jnp.where(level_ref[rows, 0:1] > 1.5, 1.0, 0.0)
        dy = (g_ref[rows, :].astype(F32) * deep * gate1).astype(BF)
        dy_ref[rows, :] = dy
        do_ref[rows, :] = nt(dy, wo[own_rows, :]).astype(BF)
        return carry

    row_blocks(some_rows)


def upstream_grads(g, level, mods, wo):
    return call(upstream_kernel, (sds((SLOTS, D), BF), sds((SLOTS, HALF), BF)), [VSPEC] * 4)(g, level, mods, wo)


def second_kernel(
    o_own_ref, o_other_ref, h_ref, level_ref, do_ref, embeds_ref, mods_ref, wq, wk, wv, wo,
    dx_ref, h1_ref, y0_ref, x_ref, o_ref, dq_ref, dk_ref, dv_ref,
    q_ref, k_ref, v_ref, lse_ref, ps, dss, bias,
):
    core = lax.axis_index("core")
    bias[...] = jnp.where(level_ref[...] > 1.5, 0.0, NEGATIVE)
    own_rows = pl.ds(pl.multiple_of(core * HALF, HALF), HALF)
    other_rows = pl.ds(pl.multiple_of((1 - core) * HALF, HALF), HALF)
    gate0 = mods_ref[2, 0:1, :]
    embed = embeds_ref[1:2, :]
    shift = mods_ref[0, 1:2, :]
    scale = 1.0 + mods_ref[1, 1:2, :]

    def forward_rows(rows):
        y0 = nn(o_own_ref[rows, :], wo[own_rows, :]) + nn(o_other_ref[rows, :], wo[other_rows, :])
        y0_ref[rows, :] = y0.astype(BF)
        h1 = (h_ref[rows, :].astype(F32) + gate0 * y0).astype(BF)
        h1_ref[rows, :] = h1
        factor, normed = norm_rows(h1.astype(F32) + embed)
        x_ref[rows, :] = (normed * scale + shift).astype(BF)

    forward_rows(pl.ds(0, BLK))
    for block in range(NBLK):
        if block + 1 < NBLK:
            forward_rows(pl.ds((block + 1) * BLK, BLK))
        rows = pl.ds(block * BLK, BLK)
        project(x_ref[rows, :], rows, wq, wk, wv, q_ref, k_ref, v_ref)
    attention_forward(q_ref, k_ref, v_ref, o_ref, lse_ref, bias)
    attention_backward(
        q_ref, k_ref, v_ref, o_ref, do_ref, lse_ref, bias, dq_ref, dk_ref, dv_ref, ps, dss
    )

    def backward_rows(rows, carry):
        dx_ref[rows, :] = unproject(rows, wq, wk, wv, dq_ref, dk_ref, dv_ref).astype(BF)
        return carry

    row_blocks(backward_rows)


def second(o_own, o_other, h, level, do, embeds, mods, wq, wk, wv, wo):
    full = sds((SLOTS, D), BF)
    half = sds((SLOTS, HALF), BF)
    scratch = pltpu.VMEM((SLOTS, HALF), BF)
    return call(
        second_kernel,
        (full, full, full, full, half, half, half, half),
        [VSPEC] * 11,
        [
            scratch, scratch, scratch, pltpu.VMEM((8, SLOTS), F32),
            pltpu.VMEM((2, SLOTS, SLOTS), BF), pltpu.VMEM((2, SLOTS, SLOTS), BF),
            pltpu.VMEM((SLOTS, 128), F32),
        ],
        20,
    )(o_own, o_other, h, level, do, embeds, mods, wq, wk, wv, wo)


def sums_kernel(x_ref, o_ref, dy_ref, dq_ref, dk_ref, dv_ref, g_ref, level_ref, wo, grads_ref, gate_ref, grads):
    core = lax.axis_index("core")
    chip = chip_index()
    own_rows = pl.ds(pl.multiple_of(core * HALF, HALF), HALF)

    def some_rows(rows, gate_sum):
        y1 = nn(o_ref[rows, :], wo[own_rows, :])
        deep = jnp.where(level_ref[rows, 0:1] > 1.5, 1.0, 0.0)
        return gate_sum + jnp.sum(g_ref[rows, :].astype(F32) * deep * y1, axis=0, keepdims=True)

    gate_sum = row_blocks(some_rows, jnp.zeros((1, D), F32))
    gate_ref[...] = jnp.broadcast_to(gate_sum, (8, D))
    weight_grads(core, chip, x_ref, o_ref, dy_ref, dq_ref, dk_ref, dv_ref, grads)
    grads_ref[...] = grads[pl.ds(pl.multiple_of((chip % 4) * 32, 32), 32), :]


def second_sums(x, o, dy, dq, dk, dv, g, level, wo):
    return call(
        sums_kernel,
        (sds((32, 5 * HALF), F32), sds((8, D), F32)),
        [VSPEC] * 9,
        [pltpu.VMEM((DH, 5 * HALF), F32)],
    )(x, o, dy, dq, dk, dv, g, level, wo)


def third_kernel(
    dx_own_ref, dx_other_ref, h1_ref, h_ref, x_ref, g_ref, level_ref, y0_ref,
    q_ref, k_ref, v_ref, o_ref, lse_ref, grads1_ref, gate1_ref, embeds_ref, mods_ref,
    wq, wk, wv, wo_ref,
    keep_ref, send_ref, mine_ref,
    dy_ref, do_ref, dq_ref, dk_ref, dv_ref, ps, dss, grads,
    bias, gs, dx0, sums,
):
    core = lax.axis_index("core")
    chip = chip_index()
    wo = wo_ref.at[pl.ds(pl.multiple_of(core * HALF, HALF), HALF)]
    bias[...] = jnp.where(level_ref[...] > 0.5, 0.0, NEGATIVE)
    scale0 = 1.0 + mods_ref[1, 0:1, :]
    gate0 = mods_ref[2, 0:1, :]
    scale1 = 1.0 + mods_ref[1, 1:2, :]
    zero = jnp.zeros((1, D), F32)

    def norm_backward(dx, u, scale):
        factor, normed = norm_rows(u)
        shift_sum = jnp.sum(dx, axis=0, keepdims=True)
        scale_sum = jnp.sum(dx * normed, axis=0, keepdims=True)
        dn = dx * scale
        du = factor * (dn - normed * jnp.mean(dn * normed, axis=-1, keepdims=True))
        return du, shift_sum, scale_sum, jnp.sum(du, axis=0, keepdims=True)

    def later_rows(rows, carry):
        shift_sum, scale_sum, embed_sum, gate_sum = carry
        dx = dx_own_ref[rows, :].astype(F32) + dx_other_ref[rows, :].astype(F32)
        u = h1_ref[rows, :].astype(F32) + embeds_ref[1:2, :]
        du, a, b, c = norm_backward(dx, u, scale1)
        shift_sum, scale_sum, embed_sum = shift_sum + a, scale_sum + b, embed_sum + c
        g = g_ref[rows, :].astype(F32) + du
        gs[rows, :] = g
        gate_sum += jnp.sum(g * y0_ref[rows, :].astype(F32), axis=0, keepdims=True)
        dy = (g * gate0).astype(BF)
        dy_ref[rows, :] = dy
        do_ref[rows, :] = nt(dy, wo[...]).astype(BF)
        return shift_sum, scale_sum, embed_sum, gate_sum

    shift_sum, scale_sum, embed_sum, gate_sum = row_blocks(later_rows, (zero,) * 4)
    sums[2:3, :] = 0.5 * gate_sum
    sums[3:4, :] = 0.5 * shift_sum
    sums[4:5, :] = 0.5 * scale_sum
    sums[5:6, :] = gate1_ref[0:1, :]
    sums[7:8, :] = 0.5 * embed_sum
    attention_backward(
        q_ref, k_ref, v_ref, o_ref, do_ref, lse_ref, bias, dq_ref, dk_ref, dv_ref, ps, dss
    )

    def earlier_rows(rows, carry):
        shift_sum, scale_sum, embed_sum = carry
        dx = unproject(rows, wq, wk, wv, dq_ref, dk_ref, dv_ref)
        dx0[rows, :] = dx
        u = h_ref[rows, :].astype(F32) + embeds_ref[0:1, :]
        du, a, b, c = norm_backward(dx, u, scale0)
        shift_sum, scale_sum, embed_sum = shift_sum + a, scale_sum + b, embed_sum + c
        return shift_sum, scale_sum, embed_sum

    shift_sum, scale_sum, embed_sum = row_blocks(earlier_rows, (zero,) * 3)
    sums[0:1, :] = shift_sum
    sums[1:2, :] = scale_sum
    sums[6:7, :] = embed_sum
    weight_grads(core, chip, x_ref, o_ref, dy_ref, dq_ref, dk_ref, dv_ref, grads)
    base = pl.multiple_of((chip % 4) * 32, 32)
    mine16 = pl.ds(pl.multiple_of(core * 16, 16), 16)
    other16 = pl.ds(pl.multiple_of((1 - core) * 16, 16), 16)
    chip_grads = grads.at[pl.ds(base, 32)]
    keep_ref[:, 0 : 5 * HALF] = (chip_grads[mine16, :] + grads1_ref[mine16, :]).astype(BF)
    send_ref[:, 0 : 5 * HALF] = (chip_grads[other16, :] + grads1_ref[other16, :]).astype(BF)
    total = jnp.concatenate([sums[:, 0:HALF], sums[:, HALF:D]], axis=0).astype(BF)
    keep_ref[:, 5 * HALF : 6 * HALF] = total
    send_ref[:, 5 * HALF : 6 * HALF] = total
    first_half = core == 0
    chip_rows = dx0.at[pl.ds(pl.multiple_of(chip * 2 * CAP, 8), 2 * CAP)]
    lower = chip_rows[0:16, :]
    upper = chip_rows[CAP - 4 : 2 * CAP, :]
    upper = jnp.concatenate([upper[4:16], upper[0:4]], axis=0)
    keep_ref[:, 6 * HALF : 8 * HALF] = jnp.where(first_half, lower, upper).astype(BF)
    send_ref[:, 6 * HALF : 8 * HALF] = jnp.where(first_half, upper, lower).astype(BF)
    g_rows = gs.at[pl.ds(pl.multiple_of(chip * 2 * CAP, 8), 2 * CAP)]
    mine_ref[...] = jnp.where(first_half, g_rows[0:CAP, :], g_rows[CAP : 2 * CAP, :])


def third(dx_own, dx_other, h1, h, x, g, level, y0, q, k, v, o, lse, grads1, gate1, embeds, mods, wq, wk, wv, wo):
    packed = sds((16, 8 * HALF), BF)
    half = pltpu.VMEM((SLOTS, HALF), BF)
    return call(
        third_kernel,
        (packed, packed, sds((CAP, D), F32)),
        [VSPEC] * 21,
        [
            pltpu.VMEM((SLOTS, D), BF), half, half, half, half,
            pltpu.VMEM((2, SLOTS, SLOTS), BF), pltpu.VMEM((2, SLOTS, SLOTS), BF),
            pltpu.VMEM((DH, 5 * HALF), F32), pltpu.VMEM((SLOTS, 128), F32),
            pltpu.VMEM((SLOTS, D), F32), pltpu.VMEM((SLOTS, D), F32), pltpu.VMEM((8, D), F32),
        ],
        28,
    )(dx_own, dx_other, h1, h, x, g, level, y0, q, k, v, o, lse, grads1, gate1, embeds, mods, wq, wk, wv, wo)


def join_kernel(keep_ref, other_ref, left_ref, right_ref):
    core = lax.axis_index("core")
    for part, (out, start) in enumerate(((left_ref, 0), (left_ref, D), (right_ref, 0))):
        cols = slice(part * HALF, (part + 1) * HALF)
        out[:, pl.ds(pl.multiple_of(start + core * HALF, HALF), HALF)] = keep_ref[:, cols]
        out[:, pl.ds(pl.multiple_of(start + (1 - core) * HALF, HALF), HALF)] = other_ref[:, cols]
    shared = slice(3 * HALF, 6 * HALF)
    both = (keep_ref[:, shared].astype(F32) + other_ref[:, shared].astype(F32)).astype(BF)
    right_ref[:, D : 2 * D] = both[:, 0:D]
    left_ref[:, 2 * D :] = both[:, D : D + 256]
    right_ref[:, 2 * D :] = both[:, D + 256 :]


def join(keep, other):
    half = sds((16, 2 * D + 256), BF)
    return call(join_kernel, (half, half), [VSPEC, VSPEC])(keep, other)


def hidden_kernel(keep_ref, other_ref, mine_ref, rows_ref, picker_ref, cot_ref, embeds_ref, mods_ref, out_ref):
    cols = slice(6 * HALF, 8 * HALF)
    dx = keep_ref[:, cols].astype(F32) + other_ref[:, cols].astype(F32)
    dx = dx[0:CAP]
    factor, normed = norm_rows(rows_ref[...].astype(F32)[0:CAP] + embeds_ref[0:1, :])
    dn = dx * (1.0 + mods_ref[1, 0:1, :])
    du = factor * (dn - normed * jnp.mean(dn * normed, axis=-1, keepdims=True))
    rows = jnp.concatenate([mine_ref[...] + du, jnp.zeros((16 - CAP, D), F32)], axis=0).astype(BF)
    picker = picker_ref[...]
    placed = tn(picker, rows)
    taken = tn(picker, jnp.ones((16, 128), BF))
    taken = jnp.concatenate([taken] * 8, axis=1)
    out_ref[0] = jnp.where(taken > 0.5, placed.astype(BF), cot_ref[0])


def hidden_grad(keep, other, mine, rows, picker, cot, embeds, mods):
    specs = [VSPEC] * 5 + [LOAD] + [VSPEC] * 2
    return call(hidden_kernel, (sds((1, TOK, D), BF),), specs, pinned=False)(
        keep, other, mine, rows, picker, cot, embeds, mods
    )[0]


def swap_cores(x):
    return lax.ppermute(x, "core", [(0, 1), (1, 0)])


def chip_index():
    return (lax.axis_index("zl") * 4 + lax.axis_index("x")) * 4 + lax.axis_index("y")


def sequence_work(gathered, rows, picker, cot, embeds, mods, weights):
    wq, wk, wv, wo = weights
    mods = mods.transpose(1, 0, 2)
    other = swap_cores(gathered)
    q, k, v, o, lse, h, g, level, x, wq, wk, wv, wo = first(gathered, other, embeds, mods, wq, wk, wv, wo)
    o_other = swap_cores(o)
    dy1, do1 = upstream_grads(g, level, mods, wo)
    dx, h1, y0, x1, o1, dq1, dk1, dv1 = second(o, o_other, h, level, do1, embeds, mods, wq, wk, wv, wo)
    dx_other = swap_cores(dx)
    grads1, gate1 = second_sums(x1, o1, dy1, dq1, dk1, dv1, g, level, wo)
    keep, send, mine = third(
        dx, dx_other, h1, h, x, g, level, y0, q, k, v, o, lse, grads1, gate1, embeds, mods, wq, wk, wv, wo
    )
    received = swap_cores(send)
    joined = join(keep, received)
    hidden = hidden_grad(keep, received, mine, rows, picker, cot, embeds, mods)
    return joined, hidden


def pair_kernel(left_ref, left_other_ref, right_ref, right_other_ref, left_out, right_out):
    left_out[...] = (left_ref[...].astype(F32) + left_other_ref[...].astype(F32)).astype(BF)
    right_out[...] = (right_ref[...].astype(F32) + right_other_ref[...].astype(F32)).astype(BF)


def final_kernel(left_ref, left_other_ref, right_ref, right_other_ref, gq_ref, gk_ref, gv_ref, go_ref, embeds_ref, mods_ref):
    left = left_ref[...].astype(F32) + left_other_ref[...].astype(F32)
    right = right_ref[...].astype(F32) + right_other_ref[...].astype(F32)
    gq_ref[...] = left[:, 0:D]
    gk_ref[...] = left[:, D : 2 * D]
    gv_ref[...] = right[:, 0:D]
    go_ref[...] = right[:, D : 2 * D]
    rest = jnp.concatenate([left[:, 2 * D :], right[:, 2 * D :]], axis=1)
    sums = jnp.concatenate([rest[0:8], rest[8:16]], axis=1)
    for kind in range(3):
        for section in range(2):
            row = 3 * section + kind
            mods_ref[kind, section : section + 1, :] = sums[row : row + 1]
    embeds_ref[...] = sums[6:8]


def dp_sum(left, right):
    def swap(x, far):
        return lax.ppermute(x, "dp", [(i, i ^ far) for i in range(4)])

    half = sds(left.shape, BF)
    left, right = call(pair_kernel, (half, half), [VSPEC] * 4)(left, swap(left, 1), right, swap(right, 3))
    block = sds((16, D), F32)
    return call(
        final_kernel,
        (block, block, block, block, sds((2, D), F32), sds((3, 2, D), F32)),
        [VSPEC] * 4,
        pinned=False,
    )(left, swap(left, 3), right, swap(right, 1))


def shards(hidden, depth, cotangent, embeds, mods, w_query, w_key, w_value, w_out):
    payload, picker, rows = pick(depth, hidden, cotangent)
    spread = jnp.broadcast_to(payload[None], (CHIPS, PACKED, 128))
    gathered = lax.all_to_all(spread, ("zl", "x", "y"), 0, 0, tiled=True)
    joined, grad_hidden = sequence_work(
        gathered, rows, picker, cotangent, embeds, mods, (w_query, w_key, w_value, w_out)
    )
    gq, gk, gv, go, grad_embeds, grad_mods = dp_sum(*joined)
    return (grad_hidden, gq, gk, gv, go, grad_embeds, grad_mods.transpose(1, 0, 2))


def solution(mesh):
    split = Mesh(mesh.devices.reshape(2, 4, 4, 2, 4), ("zl", "x", "y", "core", "dp"))
    ctx = ("zl", "x", "y", "core")
    in_specs = (P("dp", ctx, None), P("dp", ctx), P("dp", ctx, None)) + (P(),) * 6
    out_specs = (P("dp", ctx, None),) + (P(ctx, None),) * 4 + (P(), P())
    return jax.shard_map(shards, mesh=split, in_specs=in_specs, out_specs=out_specs, check_vma=False)
```

profile of v0, /device:TPU:2, one launch (start us, length us, event | category | flops | bytes accessed | tf_op | source)
XLA Modules:
  0.0 101.2 jit_solution(8509618784684142145)
XLA Ops:
  0.6 1.3 %shard_map.144 = (bf16[200,128]{1,0:T(8,128)(2,1)S(1)}, bf16[16,128]{1,0:T(8,128)(2,1)S(1)}, bf16[16,1024]{1,0:T(8,128)(2,1)S(1)}) custom-call(s32[1,128]{1,0:T(1,128)} %depth_ref.1, bf16[1,128,1024]{2,1,0:T(8,128)(2,1)} %hidden_ref.1, bf16[1,128,1024]{2,1,0:T(8,128)(2,1)} %cot_ref.3), custom_call_target="tpu_custom_call" | custom-call | tf_op jit(solution)/shard_map/pallas_call | solution.py:67
  2.0 0.2 broadcast_in_dim.2
  2.2 0.0 copy-start
  2.2 0.0 copy-start.1
  2.2 31.0 %all_to_all.5.own_ref = bf16[32,200,128]{2,1,0:T(8,128)(2,1)S(1)} all-to-all(bf16[32,200,128]{2,1,0:T(8,128)(2,1)S(1)} %broadcast_in_dim.2), channel_id=1, replica_groups=mesh['zl'=2,'x'=4,'y'=4,'core'=2,'dp'=4] {'zl','x','y'}, dimensions={0} | all-to-all | bytes 3276800 | tf_op jit(solution)/shard_map/all_to_all | solution.py:643
  33.2 0.0 collective-permute-start
  33.2 3.5 %collective-permute-done.other_ref = bf16[32,200,128]{2,1,0:T(8,128)(2,1)S(1)} collective-permute-done((bf16[32,200,128]{2,1,0:T(8,128)(2,1)S(1)}, bf16[32,200,128]{2,1,0:T(8,128)(2,1)S(1)}, u32[]{:S(2)}, u32[]{:S(2)}) %collective-permute-start) | collective-permute-done | bytes 1638432 | tf_op jit(solution)/shard_map/ppermute | solution.py:578
  36.7 0.0 copy-done
  36.7 0.0 copy-done.1
  36.7 8.5 %shard_map.145 = (bf16[768,512]{1,0:T(8,128)(2,1)S(1)}, bf16[768,512]{1,0:T(8,128)(2,1)S(1)}, bf16[768,512]{1,0:T(8,128)(2,1)S(1)}, bf16[768,512]{1,0:T(8,128)(2...) custom-call(bf16[32,200,128]{2,1,0:T(8,128)(2,1)S(1)} %all_to_all.5., ...), custom_call_target="tpu_custom_call" | custom-call | tf_op jit(solution)/shard_map/pallas_call | solution.py:67
  45.2 0.4 collective-permute-start.1
  45.6 1.6 %shard_map.146 = (bf16[768,1024]{1,0:T(8,128)(2,1)S(1)}, bf16[768,512]{1,0:T(8,128)(2,1)S(1)}) custom-call(bf16[768,1024]{1,0:T(8,128)(2,1)S(1)} %get-tuple-element.52.g_ref, f32[768,128]{1,0:T(8,128)S(1)} %get-tuple-element.51.level_ref, f32[3,2,1024]{2,1,0:T(2,128)S(1)} %bitcast.3, bf16[1024,1024]{1,0:T(8,128)(2,1)S(1)} %get-tuple-element.53.wo.wo_ref), custom_call_target="tpu_custom_call" | custom-call | tf_op jit(solution)/shard_map/pallas_call | solution.py:67
  47.2 0.6 collective-permute-done.1.o_other_ref
  47.8 14.5 %shard_map.147 = (bf16[768,1024]{1,0:T(8,128)(2,1)S(1)}, bf16[768,1024]{1,0:T(8,128)(2,1)S(1)}, bf16[768,1024]{1,0:T(8,128)(2,1)S(1)}, bf16[768,1024]{1,0:T(8,12...) custom-call(bf16[768,512]{1,0:T(8,128)(2,1)S(1)} %get-tuple-element., ...), custom_call_target="tpu_custom_call" | custom-call | tf_op jit(solution)/shard_map/pallas_call | solution.py:67
  62.2 0.4 collective-permute-start.2
  62.7 2.1 %shard_map.148 = (f32[32,2560]{1,0:T(8,128)S(1)}, f32[8,1024]{1,0:T(8,128)S(1)}) custom-call(bf16[768,1024]{1,0:T(8,128)(2,1)S(1)} %get-tuple-element.66.x_ref, bf16[768,512]{1,0:T(8,128)(2,1)S(1)} %get-tuple-element.67.o_ref, bf16[768,1024]{1,0:T(8,128)(2,1)S(1)} %get-tuple-element.68.dy_ref, bf16[768,512]{1,0:T(8,128)(2,1)S(1)} %get-tuple-element.69.dq_ref, ...), custom_call_target="tpu_custom_call" | custom-call | tf_op jit(solution)/shard_map/pallas_call | solution.py:67
  64.8 1.2 %collective-permute-done.2.dx_other_ref = bf16[768,1024]{1,0:T(8,128)(2,1)S(1)} collective-permute-done((bf16[768,1024]{1,0:T(8,128)(2,1)S(1)}, bf16[768,1024]{1,0:T(8,128)(2,1)S(1)}, u32[]{:S(2)}, u32[]{:S(2)}) %collective-permute-start.2) | collective-permute-done | bytes 1572896 | tf_op jit(solution)/shard_map/ppermute | solution.py:578
  65.9 12.6 %shard_map.149 = (bf16[16,4096]{1,0:T(8,128)(2,1)S(1)}, bf16[16,4096]{1,0:T(8,128)(2,1)S(1)}, f32[12,1024]{1,0:T(8,128)S(1)}) custom-call(bf16[768,1024]{1,0:T(8,128)(2,1)S(1)} %get-tuple-element.58.dx_own_ref, bf16[768,1024]{1,0:T(8,128)(2,1)S(1)} %collective-permute-done.2.dx_other_ref, bf16[768,1024]{1,0:T(8,128)(2,1)S(1)} %get-tuple-element.59.h1_ref, ...), custom_call_target="tpu_custom_call" | custom-call | tf_op jit(solution)/shard_map/pallas_call | solution.py:67
  78.6 0.2 collective-permute-start.3
  78.8 1.2 %collective-permute-done.3.other_ref = bf16[16,4096]{1,0:T(8,128)(2,1)S(1)} collective-permute-done((bf16[16,4096]{1,0:T(8,128)(2,1)S(1)}, bf16[16,4096]{1,0:T(8,128)(2,1)S(1)}, u32[]{:S(2)}, u32[]{:S(2)}) %collective-permute-start.3) | collective-permute-done | bytes 131104 | tf_op jit(solution)/shard_map/ppermute | solution.py:578
  80.0 3.4 %collective-permute-start.4 = (bf16[16,2304]{1,0:T(8,128)(2,1)S(1)}, bf16[16,2304]{1,0:T(8,128)(2,1)S(1)}, u32[]{:S(2)}, u32[]{:S(2)}) collective-permute-start(bf16[16,2304]{1,0:T(8,128)(2,1)S(1)} %get-tuple-element.79.left_ref), channel_id=1, source_target_pairs={{0,1},{1,0},{2,3},{3,2},{4,5},{5,4},{6,7},{7,6},{8,9},{9,8},{10,11... | collective-permute-start | bytes 221192 | tf_op jit(solution)/shard_map/ppermute | solution.py:627
  83.4 3.6 %collective-permute-start.5 = (bf16[16,2304]{1,0:T(8,128)(2,1)S(1)}, bf16[16,2304]{1,0:T(8,128)(2,1)S(1)}, u32[]{:S(2)}, u32[]{:S(2)}) collective-permute-start(bf16[16,2304]{1,0:T(8,128)(2,1)S(1)} %get-tuple-element.80.right_ref), channel_id=1, source_target_pairs={{0,3},{1,2},{2,1},{3,0},{4,7},{5,6},{6,5},{7,4},{8,11},{9,10},{10,... | collective-permute-start | bytes 221192 | tf_op jit(solution)/shard_map/ppermute | solution.py:627
  87.0 0.6 collective-permute-done.4.left_other_ref
  87.5 2.6 %collective-permute-done.5.right_other_ref = bf16[16,2304]{1,0:T(8,128)(2,1)S(1)} collective-permute-done((bf16[16,2304]{1,0:T(8,128)(2,1)S(1)}, bf16[16,2304]{1,0:T(8,128)(2,1)S(1)}, u32[]{:S(2)}, u32[]{:S(2)}) %collective-permute-start.5) | collective-permute-done | bytes 73760 | tf_op jit(solution)/shard_map/ppermute | solution.py:627
  90.2 4.6 %collective-permute-start.6 = (bf16[16,2304]{1,0:T(8,128)(2,1)S(1)}, bf16[16,2304]{1,0:T(8,128)(2,1)S(1)}, u32[]{:S(2)}, u32[]{:S(2)}) collective-permute-start(bf16[16,2304]{1,0:T(8,128)(2,1)S(1)} %get-tuple-element.81.left_ref), channel_id=1, source_target_pairs={{0,3},{1,2},{2,1},{3,0},{4,7},{5,6},{6,5},{7,4},{8,11},{9,10},{10,... | collective-permute-start | bytes 221192 | tf_op jit(solution)/shard_map/ppermute | solution.py:627
  94.8 0.5 collective-permute-start.7
  95.3 2.1 %shard_map.150 = bf16[1,128,1024]{2,1,0:T(8,128)(2,1)} custom-call(bf16[16,4096]{1,0:T(8,128)(2,1)S(1)} %get-tuple-element.74.keep_ref, bf16[16,4096]{1,0:T(8,128)(2,1)S(1)} %collective-permute-done.3.other_ref, f32[12,1024]{1,0:T(8,128)S(1)} %get-tuple-element.76.mine_ref, bf16[16,1024]{1,0:T(8,128)(2,1)S(1)} %get-tuple-element.77.rows_ref, ...), custom_call_target="tpu_custom_call" | custom-call | tf_op jit(solution)/shard_map/pallas_call | solution.py:67
  97.4 0.0 collective-permute-done.6.left_other_ref
  97.4 3.1 %collective-permute-done.7.right_other_ref = bf16[16,2304]{1,0:T(8,128)(2,1)S(1)} collective-permute-done((bf16[16,2304]{1,0:T(8,128)(2,1)S(1)}, bf16[16,2304]{1,0:T(8,128)(2,1)S(1)}, u32[]{:S(2)}, u32[]{:S(2)}) %collective-permute-start.7) | collective-permute-done | bytes 73760 | tf_op jit(solution)/shard_map/ppermute | solution.py:627
  100.5 0.7 shard_map.153
  (2 shorter events, 0.1 us)
Async XLA Ops:
  2.2 34.5 %copy-start = (f32[2,3,1024]{2,0,1:T(2,128)S(1)}, f32[2,3,1024]{2,0,1:T(2,128)}, u32[]{:S(2)}) copy-start(f32[2,3,1024]{2,0,1:T(2,128)} %param.13) | copy-start | bytes 73732
  2.2 34.5 %copy-start.1 = (f32[2,1024]{1,0:T(2,128)S(1)}, f32[2,1024]{1,0:T(2,128)}, u32[]{:S(2)}) copy-start(f32[2,1024]{1,0:T(2,128)} %embeds_ref.7) | copy-start | bytes 24580
  33.2 3.5 %collective-permute-start = (bf16[32,200,128]{2,1,0:T(8,128)(2,1)S(1)}, bf16[32,200,128]{2,1,0:T(8,128)(2,1)S(1)}, u32[]{:S(2)}, u32[]{:S(2)}) collective-permute-start(bf16[32,200,128]{2,1,0:T(8,128)(2,1)S(1)} %all_to_all.5.own_ref), channel_id=1, source_target_pairs={{0,4},{4,0},{1,5},{5,1},{2,6},{6,2},{3,7},{7,3},{8,12},{12,8},{9,1... | collective-permute-start | bytes 4915208 | tf_op jit(solution)/shard_map/ppermute | solution.py:578
  45.2 2.6 %collective-permute-start.1 = (bf16[768,512]{1,0:T(8,128)(2,1)S(1)}, bf16[768,512]{1,0:T(8,128)(2,1)S(1)}, u32[]{:S(2)}, u32[]{:S(2)}) collective-permute-start(bf16[768,512]{1,0:T(8,128)(2,1)S(1)} %get-tuple-element.49.o_own_ref.o_ref), channel_id=1, source_target_pairs={{0,4},{4,0},{1,5},{5,1},{2,6},{6,2},{3,7},{7,3},{8,12},{12,8},{9,1... | collective-permute-start | bytes 2359304 | tf_op jit(solution)/shard_map/ppermute | solution.py:578
  62.2 3.7 %collective-permute-start.2 = (bf16[768,1024]{1,0:T(8,128)(2,1)S(1)}, bf16[768,1024]{1,0:T(8,128)(2,1)S(1)}, u32[]{:S(2)}, u32[]{:S(2)}) collective-permute-start(bf16[768,1024]{1,0:T(8,128)(2,1)S(1)} %get-tuple-element.58.dx_own_ref), channel_id=1, source_target_pairs={{0,4},{4,0},{1,5},{5,1},{2,6},{6,2},{3,7},{7,3},{8,12},{12,8},{9,1... | collective-permute-start | bytes 4718600 | tf_op jit(solution)/shard_map/ppermute | solution.py:578
  78.6 1.4 %collective-permute-start.3 = (bf16[16,4096]{1,0:T(8,128)(2,1)S(1)}, bf16[16,4096]{1,0:T(8,128)(2,1)S(1)}, u32[]{:S(2)}, u32[]{:S(2)}) collective-permute-start(bf16[16,4096]{1,0:T(8,128)(2,1)S(1)} %get-tuple-element.75), channel_id=1, source_target_pairs={{0,4},{4,0},{1,5},{5,1},{2,6},{6,2},{3,7},{7,3},{8,12},{12,8},{9,1... | collective-permute-start | bytes 393224 | tf_op jit(solution)/shard_map/ppermute | solution.py:578
  80.0 7.5 %collective-permute-start.4 = (bf16[16,2304]{1,0:T(8,128)(2,1)S(1)}, bf16[16,2304]{1,0:T(8,128)(2,1)S(1)}, u32[]{:S(2)}, u32[]{:S(2)}) collective-permute-start(bf16[16,2304]{1,0:T(8,128)(2,1)S(1)} %get-tuple-element.79.left_ref), channel_id=1, source_target_pairs={{0,1},{1,0},{2,3},{3,2},{4,5},{5,4},{6,7},{7,6},{8,9},{9,8},{10,11... | collective-permute-start | bytes 221192 | tf_op jit(solution)/shard_map/ppermute | solution.py:627
  83.4 6.7 %collective-permute-start.5 = (bf16[16,2304]{1,0:T(8,128)(2,1)S(1)}, bf16[16,2304]{1,0:T(8,128)(2,1)S(1)}, u32[]{:S(2)}, u32[]{:S(2)}) collective-permute-start(bf16[16,2304]{1,0:T(8,128)(2,1)S(1)} %get-tuple-element.80.right_ref), channel_id=1, source_target_pairs={{0,3},{1,2},{2,1},{3,0},{4,7},{5,6},{6,5},{7,4},{8,11},{9,10},{10,... | collective-permute-start | bytes 221192 | tf_op jit(solution)/shard_map/ppermute | solution.py:627
  90.2 7.2 %collective-permute-start.6 = (bf16[16,2304]{1,0:T(8,128)(2,1)S(1)}, bf16[16,2304]{1,0:T(8,128)(2,1)S(1)}, u32[]{:S(2)}, u32[]{:S(2)}) collective-permute-start(bf16[16,2304]{1,0:T(8,128)(2,1)S(1)} %get-tuple-element.81.left_ref), channel_id=1, source_target_pairs={{0,3},{1,2},{2,1},{3,0},{4,7},{5,6},{6,5},{7,4},{8,11},{9,10},{10,... | collective-permute-start | bytes 221192 | tf_op jit(solution)/shard_map/ppermute | solution.py:627
  94.8 5.7 %collective-permute-start.7 = (bf16[16,2304]{1,0:T(8,128)(2,1)S(1)}, bf16[16,2304]{1,0:T(8,128)(2,1)S(1)}, u32[]{:S(2)}, u32[]{:S(2)}) collective-permute-start(bf16[16,2304]{1,0:T(8,128)(2,1)S(1)} %get-tuple-element.82.right_ref), channel_id=1, source_target_pairs={{0,1},{1,0},{2,3},{3,2},{4,5},{5,4},{6,7},{7,6},{8,9},{9,8},{10,11... | collective-permute-start | bytes 221192 | tf_op jit(solution)/shard_map/ppermute | solution.py:627
where the time goes:
time: 101 us
  Pallas kernels  43.4 us (43%)
  blocking collectives  31 us (31%)
  starting transfers between devices  13.1 us (13%)
  waiting for transfers between devices  12.7 us (13%)
    pallas_call x10, Pallas kernels, placed(): run(*(pltpu.with_memory_space_constraint(a, m) for a, m in zip(args, spac...  43.4 us
    all_to_all x1, blocking collectives, shards(): gathered = lax.all_to_all(spread, ('zl', 'x', 'y'), 0, 0, tiled=True)  31 us
    ppermute x4, starting transfers between devices, swap(): return lax.ppermute(x, 'dp', [(i, i ^ far) for i in range(4)])  12.1 us
    ppermute x4, waiting for transfers between devices, swap_cores(): return lax.ppermute(x, 'core', [(0, 1), (1, 0)])  6.44 us
    ppermute x4, waiting for transfers between devices, swap(): return lax.ppermute(x, 'dp', [(i, i ^ far) for i in range(4)])  6.3 us
  transfers between devices with their start and end apart: 8, of which 7 were waited for; matrix products, arithmetic and copies ran while one was open for 0% of the time, Pallas kernels for 6%

commit v1 on v0

--- a/solution.py
+++ b/solution.py
@@ -107,15 +107,20 @@
     return jnp.where(key <= query, 0.0, NEGATIVE).astype(F32)
 
 
+def fill_bias(level_ref, least):
+    lane = lax.broadcasted_iota(jnp.int32, (SLOTS, DH), 1)
+    return jnp.where((level_ref[...] > least) | (lane > 0), 0.0, NEGATIVE).astype(BF)
+
+
 def norm_rows(u):
     factor = lax.rsqrt(jnp.mean(u * u, axis=-1, keepdims=True) + EPSILON)
     return factor, u * factor
 
 
 def biased_scores(k, q, bias_ref, causal, upto):
-    s = nt(k, q)
-    bias = bias_ref[0:upto, :]
-    s = s + jnp.concatenate([bias, bias], axis=1)
+    lane = lax.broadcasted_iota(jnp.int32, (BLK, DH), 1)
+    unit = jnp.where(lane == 0, 1.0, 0.0).astype(BF)
+    s = nt(jnp.concatenate([k, bias_ref[0:upto, :]], axis=1), jnp.concatenate([q, unit], axis=1))
     last = s[upto - BLK : upto] + causal
     if upto == BLK:
         return last
@@ -159,11 +164,11 @@
             o_ref[rows, cols] = (both[0:DH] * (1.0 / total)).T.astype(BF)
             lse_ref[pl.ds(head, 1), rows] = jnp.maximum(top * SCALE2 + jnp.log2(total), -1e25)
 
-        state = start(*items[0])
+        states = [start(*item) for item in items[:2]]
         for i, item in enumerate(items):
-            following = start(*items[i + 1]) if i + 1 < len(items) else None
-            finish(*item, *state)
-            state = following
+            if i + 2 < len(items):
+                states.append(start(*items[i + 2]))
+            finish(*item, *states[i])
         return carry
 
     lax.fori_loop(0, HEADS // FORWARD_HEADS, some_heads, 0)
@@ -206,11 +211,11 @@
                 dv_ref[rows, cols] = nn(ps[slot, rows, later], do_ref[later, cols]).astype(BF)
                 dk_ref[rows, cols] = (nn(dss[slot, rows, later], q_ref[later, cols]) * SCALE).astype(BF)
 
-        state = start(*items[0])
+        states = [start(*item) for item in items[:1]]
         for i, item in enumerate(items):
-            following = start(*items[i + 1]) if i + 1 < len(items) else None
-            finish(*item, *state)
-            state = following
+            if i + 1 < len(items):
+                states.append(start(*items[i + 1]))
+            finish(*item, *states[i])
             if item[-1] == NBLK - 1:
                 close(*item[:3])
         return carry
@@ -281,7 +286,7 @@
             place_block(odd_ref, chip, base, CAP, hs, gs, level_ref)
             return carry
 
-        lax.fori_loop(0, CHIPS, one_chip, 0)
+        lax.fori_loop(0, CHIPS, one_chip, 0, unroll=4)
 
     @pl.when(core == 0)
     def _():
@@ -291,7 +296,7 @@
     def _():
         place(other_ref, own_ref)
 
-    bias[...] = jnp.where(level_ref[...] > 0.5, 0.0, NEGATIVE)
+    bias[...] = fill_bias(level_ref, 0.5)
     for copy in copies:
         copy.wait()
     embed = embeds_ref[0:1, :]
@@ -326,7 +331,7 @@
         [
             pltpu.VMEM((SLOTS, D), F32),
             pltpu.VMEM((SLOTS, D), F32),
-            pltpu.VMEM((SLOTS, 128), F32),
+            pltpu.VMEM((SLOTS, 128), BF),
             pltpu.SemaphoreType.DMA((4,)),
         ],
         16,
@@ -358,7 +363,7 @@
     q_ref, k_ref, v_ref, lse_ref, ps, dss, bias,
 ):
     core = lax.axis_index("core")
-    bias[...] = jnp.where(level_ref[...] > 1.5, 0.0, NEGATIVE)
+    bias[...] = fill_bias(level_ref, 1.5)
     own_rows = pl.ds(pl.multiple_of(core * HALF, HALF), HALF)
     other_rows = pl.ds(pl.multiple_of((1 - core) * HALF, HALF), HALF)
     gate0 = mods_ref[2, 0:1, :]
@@ -403,7 +408,7 @@
         [
             scratch, scratch, scratch, pltpu.VMEM((8, SLOTS), F32),
             pltpu.VMEM((2, SLOTS, SLOTS), BF), pltpu.VMEM((2, SLOTS, SLOTS), BF),
-            pltpu.VMEM((SLOTS, 128), F32),
+            pltpu.VMEM((SLOTS, 128), BF),
         ],
         20,
     )(o_own, o_other, h, level, do, embeds, mods, wq, wk, wv, wo)
@@ -434,30 +439,28 @@
     )(x, o, dy, dq, dk, dv, g, level, wo)
 
 
+def norm_backward(dx, u, scale):
+    factor, normed = norm_rows(u)
+    shift_sum = jnp.sum(dx, axis=0, keepdims=True)
+    scale_sum = jnp.sum(dx * normed, axis=0, keepdims=True)
+    dn = dx * scale
+    du = factor * (dn - normed * jnp.mean(dn * normed, axis=-1, keepdims=True))
+    return du, shift_sum, scale_sum, jnp.sum(du, axis=0, keepdims=True)
+
+
 def third_kernel(
-    dx_own_ref, dx_other_ref, h1_ref, h_ref, x_ref, g_ref, level_ref, y0_ref,
-    q_ref, k_ref, v_ref, o_ref, lse_ref, grads1_ref, gate1_ref, embeds_ref, mods_ref,
-    wq, wk, wv, wo_ref,
-    keep_ref, send_ref, mine_ref,
-    dy_ref, do_ref, dq_ref, dk_ref, dv_ref, ps, dss, grads,
-    bias, gs, dx0, sums,
+    dx_own_ref, dx_other_ref, h1_ref, x_ref, g_ref, level_ref, y0_ref,
+    q_ref, k_ref, v_ref, o_ref, lse_ref, grads1_ref, gate1_ref, embeds_ref, mods_ref, wo_ref,
+    keep_ref, send_ref, mine_ref, sums, dq_ref, dk_ref, dv_ref,
+    dy_ref, do_ref, ps, dss, grads, bias, gs,
 ):
     core = lax.axis_index("core")
     chip = chip_index()
     wo = wo_ref.at[pl.ds(pl.multiple_of(core * HALF, HALF), HALF)]
-    bias[...] = jnp.where(level_ref[...] > 0.5, 0.0, NEGATIVE)
-    scale0 = 1.0 + mods_ref[1, 0:1, :]
+    bias[...] = fill_bias(level_ref, 0.5)
     gate0 = mods_ref[2, 0:1, :]
     scale1 = 1.0 + mods_ref[1, 1:2, :]
     zero = jnp.zeros((1, D), F32)
-
-    def norm_backward(dx, u, scale):
-        factor, normed = norm_rows(u)
-        shift_sum = jnp.sum(dx, axis=0, keepdims=True)
-        scale_sum = jnp.sum(dx * normed, axis=0, keepdims=True)
-        dn = dx * scale
-        du = factor * (dn - normed * jnp.mean(dn * normed, axis=-1, keepdims=True))
-        return du, shift_sum, scale_sum, jnp.sum(du, axis=0, keepdims=True)
 
     def later_rows(rows, carry):
         shift_sum, scale_sum, embed_sum, gate_sum = carry
@@ -473,7 +476,9 @@
         do_ref[rows, :] = nt(dy, wo[...]).astype(BF)
         return shift_sum, scale_sum, embed_sum, gate_sum
 
-    shift_sum, scale_sum, embed_sum, gate_sum = row_blocks(later_rows, (zero,) * 4)
+    carry = row_blocks(later_rows, (zero,) * 4)
+    shift_sum, scale_sum, embed_sum, gate_sum = carry
+    sums[...] = jnp.zeros((8, D), F32)
     sums[2:3, :] = 0.5 * gate_sum
     sums[3:4, :] = 0.5 * shift_sum
     sums[4:5, :] = 0.5 * scale_sum
@@ -482,56 +487,86 @@
     attention_backward(
         q_ref, k_ref, v_ref, o_ref, do_ref, lse_ref, bias, dq_ref, dk_ref, dv_ref, ps, dss
     )
-
-    def earlier_rows(rows, carry):
-        shift_sum, scale_sum, embed_sum = carry
-        dx = unproject(rows, wq, wk, wv, dq_ref, dk_ref, dv_ref)
-        dx0[rows, :] = dx
-        u = h_ref[rows, :].astype(F32) + embeds_ref[0:1, :]
-        du, a, b, c = norm_backward(dx, u, scale0)
-        shift_sum, scale_sum, embed_sum = shift_sum + a, scale_sum + b, embed_sum + c
-        return shift_sum, scale_sum, embed_sum
-
-    shift_sum, scale_sum, embed_sum = row_blocks(earlier_rows, (zero,) * 3)
-    sums[0:1, :] = shift_sum
-    sums[1:2, :] = scale_sum
-    sums[6:7, :] = embed_sum
     weight_grads(core, chip, x_ref, o_ref, dy_ref, dq_ref, dk_ref, dv_ref, grads)
     base = pl.multiple_of((chip % 4) * 32, 32)
     mine16 = pl.ds(pl.multiple_of(core * 16, 16), 16)
     other16 = pl.ds(pl.multiple_of((1 - core) * 16, 16), 16)
     chip_grads = grads.at[pl.ds(base, 32)]
-    keep_ref[:, 0 : 5 * HALF] = (chip_grads[mine16, :] + grads1_ref[mine16, :]).astype(BF)
-    send_ref[:, 0 : 5 * HALF] = (chip_grads[other16, :] + grads1_ref[other16, :]).astype(BF)
+    keep_ref[...] = (chip_grads[mine16, :] + grads1_ref[mine16, :]).astype(BF)
+    send_ref[...] = (chip_grads[other16, :] + grads1_ref[other16, :]).astype(BF)
+    g_rows = gs.at[pl.ds(pl.multiple_of(chip * 2 * CAP, 8), 2 * CAP)]
+    mine_ref[...] = jnp.where(core == 0, g_rows[0:CAP, :], g_rows[CAP : 2 * CAP, :])
+
+
+def third(dx_own, dx_other, h1, x, g, level, y0, q, k, v, o, lse, grads1, gate1, embeds, mods, wo):
+    packed = sds((16, 5 * HALF), BF)
+    half = sds((SLOTS, HALF), BF)
+    return call(
+        third_kernel,
+        (packed, packed, sds((CAP, D), F32), sds((8, D), F32), half, half, half),
+        [VSPEC] * 17,
+        [
+            pltpu.VMEM((SLOTS, D), BF), pltpu.VMEM((SLOTS, HALF), BF),
+            pltpu.VMEM((2, SLOTS, SLOTS), BF), pltpu.VMEM((2, SLOTS, SLOTS), BF),
+            pltpu.VMEM((DH, 5 * HALF), F32), pltpu.VMEM((SLOTS, 128), BF), pltpu.VMEM((SLOTS, D), F32),
+        ],
+        24,
+    )(dx_own, dx_other, h1, x, g, level, y0, q, k, v, o, lse, grads1, gate1, embeds, mods, wo)
+
+
+def last_kernel(
+    dq_ref, dk_ref, dv_ref, h_ref, sums1_ref, embeds_ref, mods_ref, wq, wk, wv,
+    keep_ref, send_ref, dx0, sums,
+):
+    core = lax.axis_index("core")
+    chip = chip_index()
+    scale0 = 1.0 + mods_ref[1, 0:1, :]
+    zero = jnp.zeros((1, D), F32)
+
+    def unproject_rows(block):
+        rows = pl.ds(block * BLK, BLK)
+        dx0[rows, :] = unproject(rows, wq, wk, wv, dq_ref, dk_ref, dv_ref)
+
+    def earlier_rows(block, carry):
+        shift_sum, scale_sum, embed_sum = carry
+        rows = pl.ds(block * BLK, BLK)
+        dx = dx0[rows, :]
+        u = h_ref[rows, :].astype(F32) + embeds_ref[0:1, :]
+        du, a, b, c = norm_backward(dx, u, scale0)
+        return shift_sum + a, scale_sum + b, embed_sum + c
+
+    carry = (zero,) * 3
+    unproject_rows(0)
+    for block in range(NBLK):
+        if block + 1 < NBLK:
+            unproject_rows(block + 1)
+        carry = earlier_rows(block, carry)
+    shift_sum, scale_sum, embed_sum = carry
+    sums[...] = sums1_ref[...]
+    sums[0:1, :] = shift_sum
+    sums[1:2, :] = scale_sum
+    sums[6:7, :] = embed_sum
     total = jnp.concatenate([sums[:, 0:HALF], sums[:, HALF:D]], axis=0).astype(BF)
-    keep_ref[:, 5 * HALF : 6 * HALF] = total
-    send_ref[:, 5 * HALF : 6 * HALF] = total
+    keep_ref[:, 0:HALF] = total
+    send_ref[:, 0:HALF] = total
     first_half = core == 0
     chip_rows = dx0.at[pl.ds(pl.multiple_of(chip * 2 * CAP, 8), 2 * CAP)]
     lower = chip_rows[0:16, :]
     upper = chip_rows[CAP - 4 : 2 * CAP, :]
     upper = jnp.concatenate([upper[4:16], upper[0:4]], axis=0)
-    keep_ref[:, 6 * HALF : 8 * HALF] = jnp.where(first_half, lower, upper).astype(BF)
-    send_ref[:, 6 * HALF : 8 * HALF] = jnp.where(first_half, upper, lower).astype(BF)
-    g_rows = gs.at[pl.ds(pl.multiple_of(chip * 2 * CAP, 8), 2 * CAP)]
-    mine_ref[...] = jnp.where(first_half, g_rows[0:CAP, :], g_rows[CAP : 2 * CAP, :])
-
-
-def third(dx_own, dx_other, h1, h, x, g, level, y0, q, k, v, o, lse, grads1, gate1, embeds, mods, wq, wk, wv, wo):
-    packed = sds((16, 8 * HALF), BF)
-    half = pltpu.VMEM((SLOTS, HALF), BF)
+    keep_ref[:, HALF : 3 * HALF] = jnp.where(first_half, lower, upper).astype(BF)
+    send_ref[:, HALF : 3 * HALF] = jnp.where(first_half, upper, lower).astype(BF)
+
+
+def last(dq, dk, dv, h, sums1, embeds, mods, wq, wk, wv):
+    packed = sds((16, 3 * HALF), BF)
     return call(
-        third_kernel,
-        (packed, packed, sds((CAP, D), F32)),
-        [VSPEC] * 21,
-        [
-            pltpu.VMEM((SLOTS, D), BF), half, half, half, half,
-            pltpu.VMEM((2, SLOTS, SLOTS), BF), pltpu.VMEM((2, SLOTS, SLOTS), BF),
-            pltpu.VMEM((DH, 5 * HALF), F32), pltpu.VMEM((SLOTS, 128), F32),
-            pltpu.VMEM((SLOTS, D), F32), pltpu.VMEM((SLOTS, D), F32), pltpu.VMEM((8, D), F32),
-        ],
-        28,
-    )(dx_own, dx_other, h1, h, x, g, level, y0, q, k, v, o, lse, grads1, gate1, embeds, mods, wq, wk, wv, wo)
+        last_kernel,
+        (packed, packed),
+        [VSPEC] * 10,
+        [pltpu.VMEM((SLOTS, D), F32), pltpu.VMEM((8, D), F32)],
+        16,
+    )(dq, dk, dv, h, sums1, embeds, mods, wq, wk, wv)
 
 
 def join_kernel(keep_ref, other_ref, left_ref, right_ref):
@@ -540,20 +575,27 @@
         cols = slice(part * HALF, (part + 1) * HALF)
         out[:, pl.ds(pl.multiple_of(start + core * HALF, HALF), HALF)] = keep_ref[:, cols]
         out[:, pl.ds(pl.multiple_of(start + (1 - core) * HALF, HALF), HALF)] = other_ref[:, cols]
-    shared = slice(3 * HALF, 6 * HALF)
-    both = (keep_ref[:, shared].astype(F32) + other_ref[:, shared].astype(F32)).astype(BF)
-    right_ref[:, D : 2 * D] = both[:, 0:D]
-    left_ref[:, 2 * D :] = both[:, D : D + 256]
-    right_ref[:, 2 * D :] = both[:, D + 256 :]
+    shared = slice(3 * HALF, 5 * HALF)
+    both = keep_ref[:, shared].astype(F32) + other_ref[:, shared].astype(F32)
+    right_ref[:, D : 2 * D] = both.astype(BF)
 
 
 def join(keep, other):
-    half = sds((16, 2 * D + 256), BF)
+    half = sds((16, 2 * D), BF)
     return call(join_kernel, (half, half), [VSPEC, VSPEC])(keep, other)
 
 
+def total_kernel(keep_ref, other_ref, out_ref):
+    both = keep_ref[:, 0:HALF].astype(F32) + other_ref[:, 0:HALF].astype(F32)
+    out_ref[...] = both.astype(BF)
+
+
+def total(keep, other):
+    return call(total_kernel, (sds((16, HALF), BF),), [VSPEC, VSPEC])(keep, other)[0]
+
+
 def hidden_kernel(keep_ref, other_ref, mine_ref, rows_ref, picker_ref, cot_ref, embeds_ref, mods_ref, out_ref):
-    cols = slice(6 * HALF, 8 * HALF)
+    cols = slice(HALF, 3 * HALF)
     dx = keep_ref[:, cols].astype(F32) + other_ref[:, cols].astype(F32)
     dx = dx[0:CAP]
     factor, normed = norm_rows(rows_ref[...].astype(F32)[0:CAP] + embeds_ref[0:1, :])
@@ -592,29 +634,33 @@
     dx, h1, y0, x1, o1, dq1, dk1, dv1 = second(o, o_other, h, level, do1, embeds, mods, wq, wk, wv, wo)
     dx_other = swap_cores(dx)
     grads1, gate1 = second_sums(x1, o1, dy1, dq1, dk1, dv1, g, level, wo)
-    keep, send, mine = third(
-        dx, dx_other, h1, h, x, g, level, y0, q, k, v, o, lse, grads1, gate1, embeds, mods, wq, wk, wv, wo
+    keep, send, mine, sums1, dq0, dk0, dv0 = third(
+        dx, dx_other, h1, x, g, level, y0, q, k, v, o, lse, grads1, gate1, embeds, mods, wo
     )
-    received = swap_cores(send)
-    joined = join(keep, received)
-    hidden = hidden_grad(keep, received, mine, rows, picker, cot, embeds, mods)
-    return joined, hidden
-
-
-def pair_kernel(left_ref, left_other_ref, right_ref, right_other_ref, left_out, right_out):
-    left_out[...] = (left_ref[...].astype(F32) + left_other_ref[...].astype(F32)).astype(BF)
+    left, right = join(keep, swap_cores(send))
+    keep_rows, send_rows = last(dq0, dk0, dv0, h, sums1, embeds, mods, wq, wk, wv)
+    other_rows = swap_cores(send_rows)
+    hidden = hidden_grad(keep_rows, other_rows, mine, rows, picker, cot, embeds, mods)
+    return left, right, total(keep_rows, other_rows), hidden
+
+
+def pair_kernel(left_ref, left_other_ref, right_ref, right_other_ref, sums_ref, sums_other_ref, left_out, right_out):
+    left_out[:, 0 : 2 * D] = (left_ref[...].astype(F32) + left_other_ref[...].astype(F32)).astype(BF)
+    left_out[:, 2 * D :] = (sums_ref[...].astype(F32) + sums_other_ref[...].astype(F32)).astype(BF)
     right_out[...] = (right_ref[...].astype(F32) + right_other_ref[...].astype(F32)).astype(BF)
 
 
-def final_kernel(left_ref, left_other_ref, right_ref, right_other_ref, gq_ref, gk_ref, gv_ref, go_ref, embeds_ref, mods_ref):
+def final_kernel(
+    left_ref, left_other_ref, right_ref, right_other_ref,
+    gq_ref, gk_ref, gv_ref, go_ref, embeds_ref, mods_ref,
+):
     left = left_ref[...].astype(F32) + left_other_ref[...].astype(F32)
     right = right_ref[...].astype(F32) + right_other_ref[...].astype(F32)
     gq_ref[...] = left[:, 0:D]
     gk_ref[...] = left[:, D : 2 * D]
     gv_ref[...] = right[:, 0:D]
     go_ref[...] = right[:, D : 2 * D]
-    rest = jnp.concatenate([left[:, 2 * D :], right[:, 2 * D :]], axis=1)
-    sums = jnp.concatenate([rest[0:8], rest[8:16]], axis=1)
+    sums = jnp.concatenate([left[0:8, 2 * D :], left[8:16, 2 * D :]], axis=1)
     for kind in range(3):
         for section in range(2):
             row = 3 * section + kind
@@ -622,12 +668,13 @@
     embeds_ref[...] = sums[6:8]
 
 
-def dp_sum(left, right):
+def dp_sum(left, right, sums):
     def swap(x, far):
         return lax.ppermute(x, "dp", [(i, i ^ far) for i in range(4)])
 
-    half = sds(left.shape, BF)
-    left, right = call(pair_kernel, (half, half), [VSPEC] * 4)(left, swap(left, 1), right, swap(right, 3))
+    left, right = call(pair_kernel, (sds((16, 2 * D + HALF), BF), sds((16, 2 * D), BF)), [VSPEC] * 6)(
+        left, swap(left, 1), right, swap(right, 3), sums, swap(sums, 1)
+    )
     block = sds((16, D), F32)
     return call(
         final_kernel,
@@ -641,10 +688,10 @@
     payload, picker, rows = pick(depth, hidden, cotangent)
     spread = jnp.broadcast_to(payload[None], (CHIPS, PACKED, 128))
     gathered = lax.all_to_all(spread, ("zl", "x", "y"), 0, 0, tiled=True)
-    joined, grad_hidden = sequence_work(
+    left, right, sums, grad_hidden = sequence_work(
         gathered, rows, picker, cotangent, embeds, mods, (w_query, w_key, w_value, w_out)
     )
-    gq, gk, gv, go, grad_embeds, grad_mods = dp_sum(*joined)
+    gq, gk, gv, go, grad_embeds, grad_mods = dp_sum(left, right, sums)
     return (grad_hidden, gq, gk, gv, go, grad_embeds, grad_mods.transpose(1, 0, 2))
 
 

time: 101 us -> 98.9 us (0.979)
  Pallas kernels: 43.4 us -> 41.9 us
    pallas_call x10 -> x12, Pallas kernels: 43.4 us -> 41.9 us  [placed(): run(*(pltpu.with_memory_space_constraint(a, m) for a, m in zip(args, spac...]
    ppermute x4 -> x5, waiting for transfers between devices: 6.44 us -> 5.22 us  [swap_cores(): return lax.ppermute(x, 'core', [(0, 1), (1, 0)])]
    ppermute x4 -> x5, starting transfers between devices: 12.1 us -> 11.7 us  [swap(): return lax.ppermute(x, 'dp', [(i, i ^ far) for i in range(4)])]
    ppermute x4 -> x5, waiting for transfers between devices: 6.3 us -> 6.46 us  [swap(): return lax.ppermute(x, 'dp', [(i, i ^ far) for i in range(4)])]
  transfers between devices with their start and end apart: 8 -> 10, of which waited for: 7 -> 5; matrix products, arithmetic and copies ran while one was open for 0% -> 0% of each run, Pallas kernels for 6% -> 9%
where the time goes in v1:
time: 98.9 us; the launch traced here: 98.7 us
  Pallas kernels  41.9 us (42%)
  blocking collectives  31 us (31%)
  starting transfers between devices  13.2 us (13%)
  waiting for transfers between devices  11.7 us (12%)
    pallas_call x12, Pallas kernels, placed(): run(*(pltpu.with_memory_space_constraint(a, m) for a, m in zip(args, spac...  41.9 us
    all_to_all x1, blocking collectives, shards(): gathered = lax.all_to_all(spread, ('zl', 'x', 'y'), 0, 0, tiled=True)  31 us
    ppermute x5, starting transfers between devices, swap(): return lax.ppermute(x, 'dp', [(i, i ^ far) for i in range(4)])  11.7 us
    ppermute x5, waiting for transfers between devices, swap(): return lax.ppermute(x, 'dp', [(i, i ^ far) for i in range(4)])  6.46 us
    ppermute x5, waiting for transfers between devices, swap_cores(): return lax.ppermute(x, 'core', [(0, 1), (1, 0)])  5.22 us
  transfers between devices with their start and end apart: 10, of which 5 were waited for; matrix products, arithmetic and copies ran while one was open for 0% of the time, Pallas kernels for 9%

profile of v1, /device:TPU:2, one launch (start us, length us, event | category | flops | bytes accessed | tf_op | source)
XLA Modules:
  0.0 98.7 jit_solution(2227721897760345624)
XLA Ops:
  0.6 1.3 %shard_map.144 = (bf16[200,128]{1,0:T(8,128)(2,1)S(1)}, bf16[16,128]{1,0:T(8,128)(2,1)S(1)}, bf16[16,1024]{1,0:T(8,128)(2,1)S(1)}) custom-call(s32[1,128]{1,0:T(1,128)} %depth_ref.1, bf16[1,128,1024]{2,1,0:T(8,128)(2,1)} %hidden_ref.1, bf16[1,128,1024]{2,1,0:T(8,128)(2,1)} %cot_ref.3), custom_call_target="tpu_custom_call" | custom-call | tf_op jit(solution)/shard_map/pallas_call | solution.py:67
  2.0 0.2 broadcast_in_dim.2
  2.2 0.0 copy-start
  2.2 0.0 copy-start.1
  2.2 31.0 %all_to_all.5.own_ref = bf16[32,200,128]{2,1,0:T(8,128)(2,1)S(1)} all-to-all(bf16[32,200,128]{2,1,0:T(8,128)(2,1)S(1)} %broadcast_in_dim.2), channel_id=1, replica_groups=mesh['zl'=2,'x'=4,'y'=4,'core'=2,'dp'=4] {'zl','x','y'}, dimensions={0} | all-to-all | bytes 3276800 | tf_op jit(solution)/shard_map/all_to_all | solution.py:690
  33.2 0.0 collective-permute-start
  33.2 3.5 %collective-permute-done.other_ref = bf16[32,200,128]{2,1,0:T(8,128)(2,1)S(1)} collective-permute-done((bf16[32,200,128]{2,1,0:T(8,128)(2,1)S(1)}, bf16[32,200,128]{2,1,0:T(8,128)(2,1)S(1)}, u32[]{:S(2)}, u32[]{:S(2)}) %collective-permute-start) | collective-permute-done | bytes 1638432 | tf_op jit(solution)/shard_map/ppermute | solution.py:620
  36.7 0.0 copy-done
  36.7 0.0 copy-done.1
  36.7 8.0 %shard_map.145 = (bf16[768,512]{1,0:T(8,128)(2,1)S(1)}, bf16[768,512]{1,0:T(8,128)(2,1)S(1)}, bf16[768,512]{1,0:T(8,128)(2,1)S(1)}, bf16[768,512]{1,0:T(8,128)(2...) custom-call(bf16[32,200,128]{2,1,0:T(8,128)(2,1)S(1)} %all_to_all.5., ...), custom_call_target="tpu_custom_call" | custom-call | tf_op jit(solution)/shard_map/pallas_call | solution.py:67
  44.7 0.4 collective-permute-start.1
  45.1 1.6 %shard_map.146 = (bf16[768,1024]{1,0:T(8,128)(2,1)S(1)}, bf16[768,512]{1,0:T(8,128)(2,1)S(1)}) custom-call(bf16[768,1024]{1,0:T(8,128)(2,1)S(1)} %get-tuple-element.58.g_ref, f32[768,128]{1,0:T(8,128)S(1)} %get-tuple-element.57.level_ref, f32[3,2,1024]{2,1,0:T(2,128)S(1)} %bitcast.3, bf16[1024,1024]{1,0:T(8,128)(2,1)S(1)} %get-tuple-element.59.wo.wo_ref), custom_call_target="tpu_custom_call" | custom-call | tf_op jit(solution)/shard_map/pallas_call | solution.py:67
  46.7 0.6 collective-permute-done.1.o_other_ref
  47.2 14.1 %shard_map.147 = (bf16[768,1024]{1,0:T(8,128)(2,1)S(1)}, bf16[768,1024]{1,0:T(8,128)(2,1)S(1)}, bf16[768,1024]{1,0:T(8,128)(2,1)S(1)}, bf16[768,1024]{1,0:T(8,12...) custom-call(bf16[768,512]{1,0:T(8,128)(2,1)S(1)} %get-tuple-element., ...), custom_call_target="tpu_custom_call" | custom-call | tf_op jit(solution)/shard_map/pallas_call | solution.py:67
  61.4 0.4 collective-permute-start.2
  61.8 2.1 %shard_map.148 = (f32[32,2560]{1,0:T(8,128)S(1)}, f32[8,1024]{1,0:T(8,128)S(1)}) custom-call(bf16[768,1024]{1,0:T(8,128)(2,1)S(1)} %get-tuple-element.72.x_ref, bf16[768,512]{1,0:T(8,128)(2,1)S(1)} %get-tuple-element.73.o_ref, bf16[768,1024]{1,0:T(8,128)(2,1)S(1)} %get-tuple-element.74.dy_ref, bf16[768,512]{1,0:T(8,128)(2,1)S(1)} %get-tuple-element.75.dq_ref, ...), custom_call_target="tpu_custom_call" | custom-call | tf_op jit(solution)/shard_map/pallas_call | solution.py:67
  63.9 1.2 %collective-permute-done.2.dx_other_ref = bf16[768,1024]{1,0:T(8,128)(2,1)S(1)} collective-permute-done((bf16[768,1024]{1,0:T(8,128)(2,1)S(1)}, bf16[768,1024]{1,0:T(8,128)(2,1)S(1)}, u32[]{:S(2)}, u32[]{:S(2)}) %collective-permute-start.2) | collective-permute-done | bytes 1572896 | tf_op jit(solution)/shard_map/ppermute | solution.py:620
  65.1 8.3 %shard_map.149 = (bf16[16,2560]{1,0:T(8,128)(2,1)S(1)}, bf16[16,2560]{1,0:T(8,128)(2,1)S(1)}, f32[12,1024]{1,0:T(8,128)S(1)}, f32[8,1024]{1,0:T(8,128)S(1)}, bf1...) custom-call(bf16[768,1024]{1,0:T(8,128)(2,1)S(1)} %get-tuple-element.64.dx_own_ref, ...), custom_call_target="tpu_custom_call" | custom-call | tf_op jit(solution)/shard_map/pallas_call | solution.py:67
  73.4 0.2 collective-permute-start.4
  73.6 3.6 %shard_map.150 = (bf16[16,1536]{1,0:T(8,128)(2,1)S(1)}, bf16[16,1536]{1,0:T(8,128)(2,1)S(1)}) custom-call(bf16[768,512]{1,0:T(8,128)(2,1)S(1)} %get-tuple-element.80.dq_ref, bf16[768,512]{1,0:T(8,128)(2,1)S(1)} %get-tuple-element.81.dk_ref, bf16[768,512]{1,0:T(8,128)(2,1)S(1)} %get-tuple-element.82.dv_ref, bf16[768,1024]{1,0:T(8,128)(2,1)S(1)} %get-tuple-element.56.h_ref, ...), custom_call_target="tpu_custom_call" | custom-call | tf_op jit(solution)/shard_map/pallas_call | solution.py:67
  77.2 0.5 collective-permute-start.3
  77.7 0.0 collective-permute-done.4.other_ref
  77.7 3.4 %collective-permute-start.5 = (bf16[16,2048]{1,0:T(8,128)(2,1)S(1)}, bf16[16,2048]{1,0:T(8,128)(2,1)S(1)}, u32[]{:S(2)}, u32[]{:S(2)}) collective-permute-start(bf16[16,2048]{1,0:T(8,128)(2,1)S(1)} %get-tuple-element.91.left_ref), channel_id=1, source_target_pairs={{0,1},{1,0},{2,3},{3,2},{4,5},{5,4},{6,7},{7,6},{8,9},{9,8},{10,11... | collective-permute-start | bytes 196616 | tf_op jit(solution)/shard_map/ppermute | solution.py:673
  81.1 3.6 %collective-permute-start.6 = (bf16[16,2048]{1,0:T(8,128)(2,1)S(1)}, bf16[16,2048]{1,0:T(8,128)(2,1)S(1)}, u32[]{:S(2)}, u32[]{:S(2)}) collective-permute-start(bf16[16,2048]{1,0:T(8,128)(2,1)S(1)} %get-tuple-element.92.right_ref), channel_id=1, source_target_pairs={{0,3},{1,2},{2,1},{3,0},{4,7},{5,6},{6,5},{7,4},{8,11},{9,10},{10,... | collective-permute-start | bytes 196616 | tf_op jit(solution)/shard_map/ppermute | solution.py:673
  84.7 0.0 collective-permute-done.3.other_ref
  84.7 1.6 %collective-permute-start.7 = (bf16[16,512]{1,0:T(8,128)(2,1)S(1)}, bf16[16,512]{1,0:T(8,128)(2,1)S(1)}, u32[]{:S(2)}, u32[]{:S(2)}) collective-permute-start(bf16[16,512]{1,0:T(8,128)(2,1)S(1)} %shard_map.153.sums_ref), channel_id=1, source_target_pairs={{0,1},{1,0},{2,3},{3,2},{4,5},{5,4},{6,7},{7,6},{8,9},{9,8},{10,11... | collective-permute-start | bytes 49160 | tf_op jit(solution)/shard_map/ppermute | solution.py:673
  86.2 3.2 %collective-permute-done.7.sums_other_ref = bf16[16,512]{1,0:T(8,128)(2,1)S(1)} collective-permute-done((bf16[16,512]{1,0:T(8,128)(2,1)S(1)}, bf16[16,512]{1,0:T(8,128)(2,1)S(1)}, u32[]{:S(2)}, u32[]{:S(2)}) %collective-permute-start.7) | collective-permute-done | bytes 16416 | tf_op jit(solution)/shard_map/ppermute | solution.py:673
  89.4 0.0 collective-permute-done.5.left_other_ref
  89.4 0.0 collective-permute-done.6.right_other_ref
  89.4 2.7 %collective-permute-start.8 = (bf16[16,2560]{1,0:T(8,128)(2,1)S(1)}, bf16[16,2560]{1,0:T(8,128)(2,1)S(1)}, u32[]{:S(2)}, u32[]{:S(2)}) collective-permute-start(bf16[16,2560]{1,0:T(8,128)(2,1)S(1)} %get-tuple-element.93.left_ref), channel_id=1, source_target_pairs={{0,3},{1,2},{2,1},{3,0},{4,7},{5,6},{6,5},{7,4},{8,11},{9,10},{10,... | collective-permute-start | bytes 245768 | tf_op jit(solution)/shard_map/ppermute | solution.py:673
  92.1 0.5 collective-permute-start.9
  92.6 2.1 %shard_map.151 = bf16[1,128,1024]{2,1,0:T(8,128)(2,1)} custom-call(bf16[16,1536]{1,0:T(8,128)(2,1)S(1)} %get-tuple-element.84.keep_ref, bf16[16,1536]{1,0:T(8,128)(2,1)S(1)} %collective-permute-done.3.other_ref, f32[12,1024]{1,0:T(8,128)S(1)} %get-tuple-element.86.mine_ref, bf16[16,1024]{1,0:T(8,128)(2,1)S(1)} %get-tuple-element.87.rows_ref, ...), custom_call_target="tpu_custom_call" | custom-call | tf_op jit(solution)/shard_map/pallas_call | solution.py:67
  94.7 3.3 %collective-permute-done.9.right_other_ref = bf16[16,2048]{1,0:T(8,128)(2,1)S(1)} collective-permute-done((bf16[16,2048]{1,0:T(8,128)(2,1)S(1)}, bf16[16,2048]{1,0:T(8,128)(2,1)S(1)}, u32[]{:S(2)}, u32[]{:S(2)}) %collective-permute-start.9) | collective-permute-done | bytes 65568 | tf_op jit(solution)/shard_map/ppermute | solution.py:673
  98.0 0.0 collective-permute-done.8.left_other_ref
  98.0 0.7 shard_map.155
  (3 shorter events, 0.1 us)
Async XLA Ops:
  2.2 34.5 %copy-start = (f32[2,3,1024]{2,0,1:T(2,128)S(1)}, f32[2,3,1024]{2,0,1:T(2,128)}, u32[]{:S(2)}) copy-start(f32[2,3,1024]{2,0,1:T(2,128)} %param.13) | copy-start | bytes 73732
  2.2 34.5 %copy-start.1 = (f32[2,1024]{1,0:T(2,128)S(1)}, f32[2,1024]{1,0:T(2,128)}, u32[]{:S(2)}) copy-start(f32[2,1024]{1,0:T(2,128)} %embeds_ref.9) | copy-start | bytes 24580
  33.2 3.5 %collective-permute-start = (bf16[32,200,128]{2,1,0:T(8,128)(2,1)S(1)}, bf16[32,200,128]{2,1,0:T(8,128)(2,1)S(1)}, u32[]{:S(2)}, u32[]{:S(2)}) collective-permute-start(bf16[32,200,128]{2,1,0:T(8,128)(2,1)S(1)} %all_to_all.5.own_ref), channel_id=1, source_target_pairs={{0,4},{4,0},{1,5},{5,1},{2,6},{6,2},{3,7},{7,3},{8,12},{12,8},{9,1... | collective-permute-start | bytes 4915208 | tf_op jit(solution)/shard_map/ppermute | solution.py:620
  44.7 2.6 %collective-permute-start.1 = (bf16[768,512]{1,0:T(8,128)(2,1)S(1)}, bf16[768,512]{1,0:T(8,128)(2,1)S(1)}, u32[]{:S(2)}, u32[]{:S(2)}) collective-permute-start(bf16[768,512]{1,0:T(8,128)(2,1)S(1)} %get-tuple-element.55.o_own_ref.o_ref), channel_id=1, source_target_pairs={{0,4},{4,0},{1,5},{5,1},{2,6},{6,2},{3,7},{7,3},{8,12},{12,8},{9,1... | collective-permute-start | bytes 2359304 | tf_op jit(solution)/shard_map/ppermute | solution.py:620
  61.4 3.7 %collective-permute-start.2 = (bf16[768,1024]{1,0:T(8,128)(2,1)S(1)}, bf16[768,1024]{1,0:T(8,128)(2,1)S(1)}, u32[]{:S(2)}, u32[]{:S(2)}) collective-permute-start(bf16[768,1024]{1,0:T(8,128)(2,1)S(1)} %get-tuple-element.64.dx_own_ref), channel_id=1, source_target_pairs={{0,4},{4,0},{1,5},{5,1},{2,6},{6,2},{3,7},{7,3},{8,12},{12,8},{9,1... | collective-permute-start | bytes 4718600 | tf_op jit(solution)/shard_map/ppermute | solution.py:620
  73.4 4.3 %collective-permute-start.4 = (bf16[16,2560]{1,0:T(8,128)(2,1)S(1)}, bf16[16,2560]{1,0:T(8,128)(2,1)S(1)}, u32[]{:S(2)}, u32[]{:S(2)}) collective-permute-start(bf16[16,2560]{1,0:T(8,128)(2,1)S(1)} %get-tuple-element.90), channel_id=1, source_target_pairs={{0,4},{4,0},{1,5},{5,1},{2,6},{6,2},{3,7},{7,3},{8,12},{12,8},{9,1... | collective-permute-start | bytes 245768 | tf_op jit(solution)/shard_map/ppermute | solution.py:620
  77.2 7.4 %collective-permute-start.3 = (bf16[16,1536]{1,0:T(8,128)(2,1)S(1)}, bf16[16,1536]{1,0:T(8,128)(2,1)S(1)}, u32[]{:S(2)}, u32[]{:S(2)}) collective-permute-start(bf16[16,1536]{1,0:T(8,128)(2,1)S(1)} %get-tuple-element.85), channel_id=1, source_target_pairs={{0,4},{4,0},{1,5},{5,1},{2,6},{6,2},{3,7},{7,3},{8,12},{12,8},{9,1... | collective-permute-start | bytes 147464 | tf_op jit(solution)/shard_map/ppermute | solution.py:620
  77.7 11.7 %collective-permute-start.5 = (bf16[16,2048]{1,0:T(8,128)(2,1)S(1)}, bf16[16,2048]{1,0:T(8,128)(2,1)S(1)}, u32[]{:S(2)}, u32[]{:S(2)}) collective-permute-start(bf16[16,2048]{1,0:T(8,128)(2,1)S(1)} %get-tuple-element.91.left_ref), channel_id=1, source_target_pairs={{0,1},{1,0},{2,3},{3,2},{4,5},{5,4},{6,7},{7,6},{8,9},{9,8},{10,11... | collective-permute-start | bytes 196616 | tf_op jit(solution)/shard_map/ppermute | solution.py:673
  81.1 8.3 %collective-permute-start.6 = (bf16[16,2048]{1,0:T(8,128)(2,1)S(1)}, bf16[16,2048]{1,0:T(8,128)(2,1)S(1)}, u32[]{:S(2)}, u32[]{:S(2)}) collective-permute-start(bf16[16,2048]{1,0:T(8,128)(2,1)S(1)} %get-tuple-element.92.right_ref), channel_id=1, source_target_pairs={{0,3},{1,2},{2,1},{3,0},{4,7},{5,6},{6,5},{7,4},{8,11},{9,10},{10,... | collective-permute-start | bytes 196616 | tf_op jit(solution)/shard_map/ppermute | solution.py:673
  84.7 4.7 %collective-permute-start.7 = (bf16[16,512]{1,0:T(8,128)(2,1)S(1)}, bf16[16,512]{1,0:T(8,128)(2,1)S(1)}, u32[]{:S(2)}, u32[]{:S(2)}) collective-permute-start(bf16[16,512]{1,0:T(8,128)(2,1)S(1)} %shard_map.153.sums_ref), channel_id=1, source_target_pairs={{0,1},{1,0},{2,3},{3,2},{4,5},{5,4},{6,7},{7,6},{8,9},{9,8},{10,11... | collective-permute-start | bytes 49160 | tf_op jit(solution)/shard_map/ppermute | solution.py:673
  89.4 8.6 %collective-permute-start.8 = (bf16[16,2560]{1,0:T(8,128)(2,1)S(1)}, bf16[16,2560]{1,0:T(8,128)(2,1)S(1)}, u32[]{:S(2)}, u32[]{:S(2)}) collective-permute-start(bf16[16,2560]{1,0:T(8,128)(2,1)S(1)} %get-tuple-element.93.left_ref), channel_id=1, source_target_pairs={{0,3},{1,2},{2,1},{3,0},{4,7},{5,6},{6,5},{7,4},{8,11},{9,10},{10,... | collective-permute-start | bytes 245768 | tf_op jit(solution)/shard_map/ppermute | solution.py:673
  92.1 5.9 %collective-permute-start.9 = (bf16[16,2048]{1,0:T(8,128)(2,1)S(1)}, bf16[16,2048]{1,0:T(8,128)(2,1)S(1)}, u32[]{:S(2)}, u32[]{:S(2)}) collective-permute-start(bf16[16,2048]{1,0:T(8,128)(2,1)S(1)} %get-tuple-element.94.right_ref), channel_id=1, source_target_pairs={{0,1},{1,0},{2,3},{3,2},{4,5},{5,4},{6,7},{7,6},{8,9},{9,8},{10,11... | collective-permute-start | bytes 196616 | tf_op jit(solution)/shard_map/ppermute | solution.py:673

commit v2 on v1

--- a/solution.py
+++ b/solution.py
@@ -390,11 +390,9 @@
         q_ref, k_ref, v_ref, o_ref, do_ref, lse_ref, bias, dq_ref, dk_ref, dv_ref, ps, dss
     )
 
-    def backward_rows(rows, carry):
+    for block in range(NBLK):
+        rows = pl.ds(block * BLK, BLK)
         dx_ref[rows, :] = unproject(rows, wq, wk, wv, dq_ref, dk_ref, dv_ref).astype(BF)
-        return carry
-
-    row_blocks(backward_rows)
 
 
 def second(o_own, o_other, h, level, do, embeds, mods, wq, wk, wv, wo):

time: 98.9 us -> 98.4 us (level)
  transfers between devices with their start and end apart: 10 -> 10, of which waited for: 5 -> 5; matrix products, arithmetic and copies ran while one was open for 0% -> 0% of each run, Pallas kernels for 9% -> 10%
where the time goes in v2:
time: 98.4 us; the launch traced here: 98.2 us
  Pallas kernels  41.7 us (42%)
  blocking collectives  31 us (32%)
  starting transfers between devices  13.1 us (13%)
  waiting for transfers between devices  11.5 us (12%)
    pallas_call x12, Pallas kernels, placed(): run(*(pltpu.with_memory_space_constraint(a, m) for a, m in zip(args, spac...  41.7 us
    all_to_all x1, blocking collectives, shards(): gathered = lax.all_to_all(spread, ('zl', 'x', 'y'), 0, 0, tiled=True)  31 us
    ppermute x5, starting transfers between devices, swap(): return lax.ppermute(x, 'dp', [(i, i ^ far) for i in range(4)])  11.9 us
    ppermute x5, waiting for transfers between devices, swap(): return lax.ppermute(x, 'dp', [(i, i ^ far) for i in range(4)])  6.47 us
    ppermute x5, waiting for transfers between devices, swap_cores(): return lax.ppermute(x, 'core', [(0, 1), (1, 0)])  5.05 us
  transfers between devices with their start and end apart: 10, of which 5 were waited for; matrix products, arithmetic and copies ran while one was open for 0% of the time, Pallas kernels for 10%

profile of v2, /device:TPU:2, one launch (start us, length us, event | category | flops | bytes accessed | tf_op | source)
XLA Modules:
  0.0 98.2 jit_solution(2511009872449748433)
XLA Ops:
  0.6 1.3 %shard_map.144 = (bf16[200,128]{1,0:T(8,128)(2,1)S(1)}, bf16[16,128]{1,0:T(8,128)(2,1)S(1)}, bf16[16,1024]{1,0:T(8,128)(2,1)S(1)}) custom-call(s32[1,128]{1,0:T(1,128)} %depth_ref.1, bf16[1,128,1024]{2,1,0:T(8,128)(2,1)} %hidden_ref.1, bf16[1,128,1024]{2,1,0:T(8,128)(2,1)} %cot_ref.3), custom_call_target="tpu_custom_call" | custom-call | tf_op jit(solution)/shard_map/pallas_call | solution.py:67
  2.0 0.2 broadcast_in_dim.2
  2.2 0.0 copy-start
  2.2 0.0 copy-start.1
  2.2 31.0 %all_to_all.5.own_ref = bf16[32,200,128]{2,1,0:T(8,128)(2,1)S(1)} all-to-all(bf16[32,200,128]{2,1,0:T(8,128)(2,1)S(1)} %broadcast_in_dim.2), channel_id=1, replica_groups=mesh['zl'=2,'x'=4,'y'=4,'core'=2,'dp'=4] {'zl','x','y'}, dimensions={0} | all-to-all | bytes 3276800 | tf_op jit(solution)/shard_map/all_to_all | solution.py:688
  33.2 0.0 collective-permute-start
  33.2 3.5 %collective-permute-done.other_ref = bf16[32,200,128]{2,1,0:T(8,128)(2,1)S(1)} collective-permute-done((bf16[32,200,128]{2,1,0:T(8,128)(2,1)S(1)}, bf16[32,200,128]{2,1,0:T(8,128)(2,1)S(1)}, u32[]{:S(2)}, u32[]{:S(2)}) %collective-permute-start) | collective-permute-done | bytes 1638432 | tf_op jit(solution)/shard_map/ppermute | solution.py:618
  36.7 0.0 copy-done
  36.7 0.0 copy-done.1
  36.7 8.0 %shard_map.145 = (bf16[768,512]{1,0:T(8,128)(2,1)S(1)}, bf16[768,512]{1,0:T(8,128)(2,1)S(1)}, bf16[768,512]{1,0:T(8,128)(2,1)S(1)}, bf16[768,512]{1,0:T(8,128)(2...) custom-call(bf16[32,200,128]{2,1,0:T(8,128)(2,1)S(1)} %all_to_all.5., ...), custom_call_target="tpu_custom_call" | custom-call | tf_op jit(solution)/shard_map/pallas_call | solution.py:67
  44.7 0.2 collective-permute-start.1
  44.9 1.8 %shard_map.146 = (bf16[768,1024]{1,0:T(8,128)(2,1)S(1)}, bf16[768,512]{1,0:T(8,128)(2,1)S(1)}) custom-call(bf16[768,1024]{1,0:T(8,128)(2,1)S(1)} %get-tuple-element.58.g_ref, f32[768,128]{1,0:T(8,128)S(1)} %get-tuple-element.57.level_ref, f32[3,2,1024]{2,1,0:T(2,128)S(1)} %bitcast.3, bf16[1024,1024]{1,0:T(8,128)(2,1)S(1)} %get-tuple-element.59.wo.wo_ref), custom_call_target="tpu_custom_call" | custom-call | tf_op jit(solution)/shard_map/pallas_call | solution.py:67
  46.7 0.4 collective-permute-done.1.o_other_ref
  47.1 13.7 %shard_map.147 = (bf16[768,1024]{1,0:T(8,128)(2,1)S(1)}, bf16[768,1024]{1,0:T(8,128)(2,1)S(1)}, bf16[768,1024]{1,0:T(8,128)(2,1)S(1)}, bf16[768,1024]{1,0:T(8,12...) custom-call(bf16[768,512]{1,0:T(8,128)(2,1)S(1)} %get-tuple-element., ...), custom_call_target="tpu_custom_call" | custom-call | tf_op jit(solution)/shard_map/pallas_call | solution.py:67
  60.8 0.2 collective-permute-start.2
  61.0 2.1 %shard_map.148 = (f32[32,2560]{1,0:T(8,128)S(1)}, f32[8,1024]{1,0:T(8,128)S(1)}) custom-call(bf16[768,1024]{1,0:T(8,128)(2,1)S(1)} %get-tuple-element.72.x_ref, bf16[768,512]{1,0:T(8,128)(2,1)S(1)} %get-tuple-element.73.o_ref, bf16[768,1024]{1,0:T(8,128)(2,1)S(1)} %get-tuple-element.74.dy_ref, bf16[768,512]{1,0:T(8,128)(2,1)S(1)} %get-tuple-element.75.dq_ref, ...), custom_call_target="tpu_custom_call" | custom-call | tf_op jit(solution)/shard_map/pallas_call | solution.py:67
  63.1 1.2 %collective-permute-done.2.dx_other_ref = bf16[768,1024]{1,0:T(8,128)(2,1)S(1)} collective-permute-done((bf16[768,1024]{1,0:T(8,128)(2,1)S(1)}, bf16[768,1024]{1,0:T(8,128)(2,1)S(1)}, u32[]{:S(2)}, u32[]{:S(2)}) %collective-permute-start.2) | collective-permute-done | bytes 1572896 | tf_op jit(solution)/shard_map/ppermute | solution.py:618
  64.3 8.3 %shard_map.149 = (bf16[16,2560]{1,0:T(8,128)(2,1)S(1)}, bf16[16,2560]{1,0:T(8,128)(2,1)S(1)}, f32[12,1024]{1,0:T(8,128)S(1)}, f32[8,1024]{1,0:T(8,128)S(1)}, bf1...) custom-call(bf16[768,1024]{1,0:T(8,128)(2,1)S(1)} %get-tuple-element.64.dx_own_ref, ...), custom_call_target="tpu_custom_call" | custom-call | tf_op jit(solution)/shard_map/pallas_call | solution.py:67
  72.6 0.2 collective-permute-start.4
  72.9 3.6 %shard_map.150 = (bf16[16,1536]{1,0:T(8,128)(2,1)S(1)}, bf16[16,1536]{1,0:T(8,128)(2,1)S(1)}) custom-call(bf16[768,512]{1,0:T(8,128)(2,1)S(1)} %get-tuple-element.80.dq_ref, bf16[768,512]{1,0:T(8,128)(2,1)S(1)} %get-tuple-element.81.dk_ref, bf16[768,512]{1,0:T(8,128)(2,1)S(1)} %get-tuple-element.82.dv_ref, bf16[768,1024]{1,0:T(8,128)(2,1)S(1)} %get-tuple-element.56.h_ref, ...), custom_call_target="tpu_custom_call" | custom-call | tf_op jit(solution)/shard_map/pallas_call | solution.py:67
  76.4 0.5 collective-permute-start.3
  76.9 0.0 collective-permute-done.4.other_ref
  76.9 3.6 %collective-permute-start.5 = (bf16[16,2048]{1,0:T(8,128)(2,1)S(1)}, bf16[16,2048]{1,0:T(8,128)(2,1)S(1)}, u32[]{:S(2)}, u32[]{:S(2)}) collective-permute-start(bf16[16,2048]{1,0:T(8,128)(2,1)S(1)} %get-tuple-element.91.left_ref), channel_id=1, source_target_pairs={{0,1},{1,0},{2,3},{3,2},{4,5},{5,4},{6,7},{7,6},{8,9},{9,8},{10,11... | collective-permute-start | bytes 196616 | tf_op jit(solution)/shard_map/ppermute | solution.py:671
  80.5 3.6 %collective-permute-start.6 = (bf16[16,2048]{1,0:T(8,128)(2,1)S(1)}, bf16[16,2048]{1,0:T(8,128)(2,1)S(1)}, u32[]{:S(2)}, u32[]{:S(2)}) collective-permute-start(bf16[16,2048]{1,0:T(8,128)(2,1)S(1)} %get-tuple-element.92.right_ref), channel_id=1, source_target_pairs={{0,3},{1,2},{2,1},{3,0},{4,7},{5,6},{6,5},{7,4},{8,11},{9,10},{10,... | collective-permute-start | bytes 196616 | tf_op jit(solution)/shard_map/ppermute | solution.py:671
  84.1 0.0 collective-permute-done.3.other_ref
  84.1 1.6 %collective-permute-start.7 = (bf16[16,512]{1,0:T(8,128)(2,1)S(1)}, bf16[16,512]{1,0:T(8,128)(2,1)S(1)}, u32[]{:S(2)}, u32[]{:S(2)}) collective-permute-start(bf16[16,512]{1,0:T(8,128)(2,1)S(1)} %shard_map.153.sums_ref), channel_id=1, source_target_pairs={{0,1},{1,0},{2,3},{3,2},{4,5},{5,4},{6,7},{7,6},{8,9},{9,8},{10,11... | collective-permute-start | bytes 49160 | tf_op jit(solution)/shard_map/ppermute | solution.py:671
  85.7 3.2 %collective-permute-done.7.sums_other_ref = bf16[16,512]{1,0:T(8,128)(2,1)S(1)} collective-permute-done((bf16[16,512]{1,0:T(8,128)(2,1)S(1)}, bf16[16,512]{1,0:T(8,128)(2,1)S(1)}, u32[]{:S(2)}, u32[]{:S(2)}) %collective-permute-start.7) | collective-permute-done | bytes 16416 | tf_op jit(solution)/shard_map/ppermute | solution.py:671
  88.9 0.0 collective-permute-done.5.left_other_ref
  88.9 0.0 collective-permute-done.6.right_other_ref
  88.9 2.7 %collective-permute-start.8 = (bf16[16,2560]{1,0:T(8,128)(2,1)S(1)}, bf16[16,2560]{1,0:T(8,128)(2,1)S(1)}, u32[]{:S(2)}, u32[]{:S(2)}) collective-permute-start(bf16[16,2560]{1,0:T(8,128)(2,1)S(1)} %get-tuple-element.93.left_ref), channel_id=1, source_target_pairs={{0,3},{1,2},{2,1},{3,0},{4,7},{5,6},{6,5},{7,4},{8,11},{9,10},{10,... | collective-permute-start | bytes 245768 | tf_op jit(solution)/shard_map/ppermute | solution.py:671
  91.6 0.5 collective-permute-start.9
  92.1 2.1 %shard_map.151 = bf16[1,128,1024]{2,1,0:T(8,128)(2,1)} custom-call(bf16[16,1536]{1,0:T(8,128)(2,1)S(1)} %get-tuple-element.84.keep_ref, bf16[16,1536]{1,0:T(8,128)(2,1)S(1)} %collective-permute-done.3.other_ref, f32[12,1024]{1,0:T(8,128)S(1)} %get-tuple-element.86.mine_ref, bf16[16,1024]{1,0:T(8,128)(2,1)S(1)} %get-tuple-element.87.rows_ref, ...), custom_call_target="tpu_custom_call" | custom-call | tf_op jit(solution)/shard_map/pallas_call | solution.py:67
  94.2 3.3 %collective-permute-done.9.right_other_ref = bf16[16,2048]{1,0:T(8,128)(2,1)S(1)} collective-permute-done((bf16[16,2048]{1,0:T(8,128)(2,1)S(1)}, bf16[16,2048]{1,0:T(8,128)(2,1)S(1)}, u32[]{:S(2)}, u32[]{:S(2)}) %collective-permute-start.9) | collective-permute-done | bytes 65568 | tf_op jit(solution)/shard_map/ppermute | solution.py:671
  97.5 0.0 collective-permute-done.8.left_other_ref
  97.5 0.7 shard_map.155
  (3 shorter events, 0.1 us)
Async XLA Ops:
  2.2 34.5 %copy-start = (f32[2,3,1024]{2,0,1:T(2,128)S(1)}, f32[2,3,1024]{2,0,1:T(2,128)}, u32[]{:S(2)}) copy-start(f32[2,3,1024]{2,0,1:T(2,128)} %param.13) | copy-start | bytes 73732
  2.2 34.5 %copy-start.1 = (f32[2,1024]{1,0:T(2,128)S(1)}, f32[2,1024]{1,0:T(2,128)}, u32[]{:S(2)}) copy-start(f32[2,1024]{1,0:T(2,128)} %embeds_ref.9) | copy-start | bytes 24580
  33.2 3.5 %collective-permute-start = (bf16[32,200,128]{2,1,0:T(8,128)(2,1)S(1)}, bf16[32,200,128]{2,1,0:T(8,128)(2,1)S(1)}, u32[]{:S(2)}, u32[]{:S(2)}) collective-permute-start(bf16[32,200,128]{2,1,0:T(8,128)(2,1)S(1)} %all_to_all.5.own_ref), channel_id=1, source_target_pairs={{0,4},{4,0},{1,5},{5,1},{2,6},{6,2},{3,7},{7,3},{8,12},{12,8},{9,1... | collective-permute-start | bytes 4915208 | tf_op jit(solution)/shard_map/ppermute | solution.py:618
  44.7 2.4 %collective-permute-start.1 = (bf16[768,512]{1,0:T(8,128)(2,1)S(1)}, bf16[768,512]{1,0:T(8,128)(2,1)S(1)}, u32[]{:S(2)}, u32[]{:S(2)}) collective-permute-start(bf16[768,512]{1,0:T(8,128)(2,1)S(1)} %get-tuple-element.55.o_own_ref.o_ref), channel_id=1, source_target_pairs={{0,4},{4,0},{1,5},{5,1},{2,6},{6,2},{3,7},{7,3},{8,12},{12,8},{9,1... | collective-permute-start | bytes 2359304 | tf_op jit(solution)/shard_map/ppermute | solution.py:618
  60.8 3.5 %collective-permute-start.2 = (bf16[768,1024]{1,0:T(8,128)(2,1)S(1)}, bf16[768,1024]{1,0:T(8,128)(2,1)S(1)}, u32[]{:S(2)}, u32[]{:S(2)}) collective-permute-start(bf16[768,1024]{1,0:T(8,128)(2,1)S(1)} %get-tuple-element.64.dx_own_ref), channel_id=1, source_target_pairs={{0,4},{4,0},{1,5},{5,1},{2,6},{6,2},{3,7},{7,3},{8,12},{12,8},{9,1... | collective-permute-start | bytes 4718600 | tf_op jit(solution)/shard_map/ppermute | solution.py:618
  72.6 4.3 %collective-permute-start.4 = (bf16[16,2560]{1,0:T(8,128)(2,1)S(1)}, bf16[16,2560]{1,0:T(8,128)(2,1)S(1)}, u32[]{:S(2)}, u32[]{:S(2)}) collective-permute-start(bf16[16,2560]{1,0:T(8,128)(2,1)S(1)} %get-tuple-element.90), channel_id=1, source_target_pairs={{0,4},{4,0},{1,5},{5,1},{2,6},{6,2},{3,7},{7,3},{8,12},{12,8},{9,1... | collective-permute-start | bytes 245768 | tf_op jit(solution)/shard_map/ppermute | solution.py:618
  76.4 7.7 %collective-permute-start.3 = (bf16[16,1536]{1,0:T(8,128)(2,1)S(1)}, bf16[16,1536]{1,0:T(8,128)(2,1)S(1)}, u32[]{:S(2)}, u32[]{:S(2)}) collective-permute-start(bf16[16,1536]{1,0:T(8,128)(2,1)S(1)} %get-tuple-element.85), channel_id=1, source_target_pairs={{0,4},{4,0},{1,5},{5,1},{2,6},{6,2},{3,7},{7,3},{8,12},{12,8},{9,1... | collective-permute-start | bytes 147464 | tf_op jit(solution)/shard_map/ppermute | solution.py:618
  76.9 11.9 %collective-permute-start.5 = (bf16[16,2048]{1,0:T(8,128)(2,1)S(1)}, bf16[16,2048]{1,0:T(8,128)(2,1)S(1)}, u32[]{:S(2)}, u32[]{:S(2)}) collective-permute-start(bf16[16,2048]{1,0:T(8,128)(2,1)S(1)} %get-tuple-element.91.left_ref), channel_id=1, source_target_pairs={{0,1},{1,0},{2,3},{3,2},{4,5},{5,4},{6,7},{7,6},{8,9},{9,8},{10,11... | collective-permute-start | bytes 196616 | tf_op jit(solution)/shard_map/ppermute | solution.py:671
  80.5 8.3 %collective-permute-start.6 = (bf16[16,2048]{1,0:T(8,128)(2,1)S(1)}, bf16[16,2048]{1,0:T(8,128)(2,1)S(1)}, u32[]{:S(2)}, u32[]{:S(2)}) collective-permute-start(bf16[16,2048]{1,0:T(8,128)(2,1)S(1)} %get-tuple-element.92.right_ref), channel_id=1, source_target_pairs={{0,3},{1,2},{2,1},{3,0},{4,7},{5,6},{6,5},{7,4},{8,11},{9,10},{10,... | collective-permute-start | bytes 196616 | tf_op jit(solution)/shard_map/ppermute | solution.py:671
  84.1 4.7 %collective-permute-start.7 = (bf16[16,512]{1,0:T(8,128)(2,1)S(1)}, bf16[16,512]{1,0:T(8,128)(2,1)S(1)}, u32[]{:S(2)}, u32[]{:S(2)}) collective-permute-start(bf16[16,512]{1,0:T(8,128)(2,1)S(1)} %shard_map.153.sums_ref), channel_id=1, source_target_pairs={{0,1},{1,0},{2,3},{3,2},{4,5},{5,4},{6,7},{7,6},{8,9},{9,8},{10,11... | collective-permute-start | bytes 49160 | tf_op jit(solution)/shard_map/ppermute | solution.py:671
  88.9 8.6 %collective-permute-start.8 = (bf16[16,2560]{1,0:T(8,128)(2,1)S(1)}, bf16[16,2560]{1,0:T(8,128)(2,1)S(1)}, u32[]{:S(2)}, u32[]{:S(2)}) collective-permute-start(bf16[16,2560]{1,0:T(8,128)(2,1)S(1)} %get-tuple-element.93.left_ref), channel_id=1, source_target_pairs={{0,3},{1,2},{2,1},{3,0},{4,7},{5,6},{6,5},{7,4},{8,11},{9,10},{10,... | collective-permute-start | bytes 245768 | tf_op jit(solution)/shard_map/ppermute | solution.py:671
  91.6 5.9 %collective-permute-start.9 = (bf16[16,2048]{1,0:T(8,128)(2,1)S(1)}, bf16[16,2048]{1,0:T(8,128)(2,1)S(1)}, u32[]{:S(2)}, u32[]{:S(2)}) collective-permute-start(bf16[16,2048]{1,0:T(8,128)(2,1)S(1)} %get-tuple-element.94.right_ref), channel_id=1, source_target_pairs={{0,1},{1,0},{2,3},{3,2},{4,5},{5,4},{6,7},{7,6},{8,9},{9,8},{10,11... | collective-permute-start | bytes 196616 | tf_op jit(solution)/shard_map/ppermute | solution.py:671
